TPU v7x, 32 devices: a whole 2x2x4 slice. The times are simulated.
32 devices in a mesh: row: 8 (over y, x, core), col: 4 (over z).
Axes of the slice: x: 2, y: 2, z: 4, core: 2. Of those that a mesh axis runs over, the one named last changes fastest.
Arguments:
- pair_map: bfloat16 [256, 256, 128], P('row', 'col'), may hold values from -6 to 6
- token_mask: int32 [256], replicated, may hold values 0 or 1
- norm_gain: float32 [2, 128], replicated, may hold values from 0.1 to 1.9
- norm_bias: float32 [2, 128], replicated, may hold values from -3 to 3
- proj_weight: bfloat16 [2, 128, 256], replicated, may hold values from -0.5 to 0.5
- gate_weight: bfloat16 [2, 128, 256], replicated, may hold values from -0.5 to 0.5
- out_gain: float32 [2, 128], replicated, may hold values from 0.1 to 1.9
- out_bias: float32 [2, 128], replicated, may hold values from -3 to 3
- final_weight: bfloat16 [2, 128, 128], replicated, may hold values from -0.5 to 0.5
- output_gate: bfloat16 [2, 128, 128], replicated, may hold values from -0.5 to 0.5
Outputs:
- updated_pair: bfloat16 [256, 256, 128], P('row', 'col')
Inputs may be any that keep to these rules, and one draw needn't show every extreme that they name: `token_mask`: 1 marks a real token, 0 a padding token.
All inputs are finite; a program needn't handle non-finite values.
Results may differ from a plain program's by a relative error of at most 0.014.
Values may be sent and summed in bfloat16 or wider, within the bound.
No kernel may reach another device: no remote copies, remote signals or barrier semaphores. Data moves between devices by JAX's collectives and lax.ppermute only.
A program may use at most 128 MiB of HBM per device.

v0:
```python
import jax
import jax.numpy as jnp
from jax import lax
from jax.sharding import PartitionSpec as P


def normalize(values, gain_vector, bias_vector):
    average = jnp.mean(values, axis=-1, keepdims=True)
    centred = values - average
    variance = jnp.mean(centred * centred, axis=-1, keepdims=True)
    return centred * lax.rsqrt(variance + 1e-05) * gain_vector + bias_vector


def project(
    pair_map, pair_mask, norm_gain, norm_bias, proj_weight, gate_weight, output_gate, layer_id
):
    normed = normalize(
        pair_map.astype(jnp.float32), norm_gain[layer_id], norm_bias[layer_id]
    ).astype(jnp.bfloat16)
    projected = jnp.dot(normed, proj_weight[layer_id], preferred_element_type=jnp.float32)
    gating = jnp.dot(normed, gate_weight[layer_id], preferred_element_type=jnp.float32)
    halves = (jax.nn.sigmoid(gating) * projected * pair_mask[..., None]).astype(jnp.bfloat16)
    closing = jax.nn.sigmoid(
        jnp.dot(normed, output_gate[layer_id], preferred_element_type=jnp.float32)
    )
    return (halves, closing)


def finish(pair_map, summed, closing, out_gain, out_bias, final_weight, layer_id):
    lifted = normalize(summed.astype(jnp.float32), out_gain[layer_id], out_bias[layer_id]).astype(
        jnp.bfloat16
    )
    update = closing * jnp.dot(lifted, final_weight[layer_id], preferred_element_type=jnp.float32)
    return (pair_map.astype(jnp.float32) + update).astype(jnp.bfloat16)


def shards(
    pair_map,
    token_mask,
    norm_gain,
    norm_bias,
    proj_weight,
    gate_weight,
    out_gain,
    out_bias,
    final_weight,
    output_gate,
):
    rows_here = pair_map.shape[0]
    cols_here = pair_map.shape[1]
    hidden = proj_weight.shape[2] // 2
    row_mask = lax.dynamic_slice_in_dim(
        token_mask, lax.axis_index("row") * rows_here, rows_here
    ).astype(jnp.float32)
    col_mask = lax.dynamic_slice_in_dim(
        token_mask, lax.axis_index("col") * cols_here, cols_here
    ).astype(jnp.float32)
    pair_mask = row_mask[:, None] * col_mask[None, :]
    halves, closing = project(
        pair_map, pair_mask, norm_gain, norm_bias, proj_weight, gate_weight, output_gate, 0
    )
    left_side = halves[..., :hidden]
    right_side = halves[..., hidden:]
    right_rows = lax.all_gather(right_side, "row", axis=0, tiled=True)
    partial_value = jnp.einsum(
        "ikh,jkh->ijh", left_side, right_rows, preferred_element_type=jnp.float32
    )
    summed = lax.psum_scatter(partial_value, "col", scatter_dimension=1, tiled=True).astype(
        jnp.bfloat16
    )
    pair_map = finish(pair_map, summed, closing, out_gain, out_bias, final_weight, 0)
    halves, closing = project(
        pair_map, pair_mask, norm_gain, norm_bias, proj_weight, gate_weight, output_gate, 1
    )
    left_side = halves[..., :hidden]
    right_side = halves[..., hidden:]
    left_cols = lax.all_gather(left_side, "col", axis=1, tiled=True)
    partial_value = jnp.einsum(
        "kih,kjh->ijh", left_cols, right_side, preferred_element_type=jnp.float32
    )
    summed = lax.psum_scatter(partial_value, "row", scatter_dimension=0, tiled=True).astype(
        jnp.bfloat16
    )
    return finish(pair_map, summed, closing, out_gain, out_bias, final_weight, 1)


def solution(mesh):
    return jax.shard_map(
        shards,
        mesh=mesh,
        in_specs=(P("row", "col", None), P(), P(), P(), P(), P(), P(), P(), P(), P()),
        out_specs=P("row", "col", None),
        check_vma=False,
    )
```

profile of v0, /device:TPU:1, one launch (start us, length us, event | category | flops | bytes accessed | tf_op | source)
XLA Modules:
  0.0 315.1 jit_solution(18066803111816030845)
XLA Ops:
  6.5 0.8 dynamic-slice_convert_fusion
  7.4 0.8 dynamic-slice_convert_fusion.1
  8.1 1.4 convert_reduce_fusion.1
  9.5 1.7 fusion.22
  11.2 0.8 slice_bitcast_fusion.2
  12.0 0.1 add_rsqrt_fusion.3
  12.0 1.9 fusion.42
  14.0 1.1 multiply_convert_fusion.1
  15.1 1.1 fusion.68
  16.2 0.0 all-gather.3.cloned.1.call-update
  16.2 0.0 reduce-scatter.3.cloned.1.call-start
  16.3 1.6 copy.48
  17.9 37.7 %all-gather.3.cloned.1.call-done = bf16[256,64,128]{2,1,0:T(8,128)(2,1)} async-done(((bf16[32,64,128]{2,1,0:T(8,128)(2,1)}), bf16[256,64,128]{2,1,0:T(8,128)(2,1)}) %all-gather.3.cloned.1.call-update) | async-done | bytes 4194320 | tf_op jit(solution)/shard_map/all_gather | solution.py:64
  55.6 12.9 %copy.47 = bf16[256,64,128]{1,0,2:T(8,128)(2,1)} copy(bf16[256,64,128]{2,1,0:T(8,128)(2,1)} %all-gather.3.cloned.1.call-done) | data formatting | bytes 8388608 | tf_op jit(solution)/shard_map/all_gather | solution.py:64
  68.5 8.3 %convolution_bitcast_fusion.1 = f32[32,256,128]{1,0,2:T(8,128)} fusion(bf16[256,64,128]{1,0,2:T(8,128)(2,1)} %copy.47, bf16[32,64,128]{1,0,2:T(8,128)(2,1)S(1)} %copy.48), kind=kOutput, calls=%fused_computation.1 | convolution fusion | flops 134217728 | bytes 8912896 | tf_op jit(solution)/shard_map/ikh,jkh->ijh/dot_general | solution.py:65
  76.8 6.0 %copy.49 = f32[32,256,128]{2,0,1:T(8,128)} copy(f32[32,256,128]{1,0,2:T(8,128)} %convolution_bitcast_fusion.1) | data formatting | bytes 8388608 | tf_op jit(solution)/shard_map/ikh,jkh->ijh/transpose | solution.py:65
  82.8 0.0 reduce-scatter.3.cloned.1.call-update
  82.8 0.0 all-gather.5.cloned.1.call-start
  82.9 0.6 copy-done.7
  83.5 0.0 copy-done.8
  83.5 75.9 %reduce-scatter.3.cloned.1.call-done = f32[32,64,128]{2,0,1:T(8,128)} async-done(((f32[32,256,128]{2,0,1:T(8,128)}), f32[32,64,128]{2,0,1:T(8,128)}) %reduce-scatter.3.cloned.1.call-update) | async-done | bytes 1048592 | tf_op jit(solution)/shard_map/reduce_scatter | solution.py:68
  159.3 1.7 convert_reduce_fusion.3
  161.0 0.1 copy.50
  161.1 0.1 copy.51
  161.1 0.0 copy-start.10
  161.2 1.9 fusion.30
  163.1 0.1 copy.52
  163.1 0.1 copy.53
  163.2 0.6 fusion.33
  163.9 0.3 fusion.36
  164.2 1.2 convert_reduce_fusion
  165.4 0.6 fusion.18
  166.1 0.7 fusion.46
  166.8 1.1 multiply_convert_fusion
  167.9 1.1 fusion.67
  169.0 0.0 all-gather.5.cloned.1.call-update
  169.1 0.2 reduce-scatter.5.cloned.1.call-start
  169.3 1.6 copy.55
  170.9 44.7 %all-gather.5.cloned.1.call-done = bf16[32,256,128]{2,1,0:T(8,128)(2,1)} async-done(((bf16[32,64,128]{2,1,0:T(8,128)(2,1)}), bf16[32,256,128]{2,1,0:T(8,128)(2,1)}) %all-gather.5.cloned.1.call-update) | async-done | bytes 2097168 | tf_op jit(solution)/shard_map/all_gather | solution.py:77
  215.6 3.4 %copy.56 = bf16[32,256,128]{1,0,2:T(8,128)(2,1)S(1)} copy(bf16[32,256,128]{2,1,0:T(8,128)(2,1)} %all-gather.5.cloned.1.call-done) | data formatting | bytes 4194304 | tf_op jit(solution)/shard_map/all_gather | solution.py:77
  219.0 4.5 %convolution_bitcast_fusion = f32[256,64,128]{0,1,2:T(8,128)} fusion(bf16[32,64,128]{1,0,2:T(8,128)(2,1)S(1)} %copy.55, bf16[32,256,128]{1,0,2:T(8,128)(2,1)S(1)} %copy.56), kind=kOutput, calls=%fused_computation | convolution fusion | flops 134217728 | bytes 11010048 | tf_op jit(solution)/shard_map/kih,kjh->ijh/dot_general | solution.py:78
  223.5 8.9 %copy.57 = f32[256,64,128]{2,1,0:T(8,128)} copy(f32[256,64,128]{0,1,2:T(8,128)} %convolution_bitcast_fusion) | data formatting | bytes 16777216 | tf_op jit(solution)/shard_map/kih,kjh->ijh/transpose | solution.py:78
  232.4 0.0 reduce-scatter.5.cloned.1.call-update
  232.4 70.2 %reduce-scatter.5.cloned.1.call-done = f32[32,64,128]{2,1,0:T(8,128)} async-done(((f32[256,64,128]{2,1,0:T(8,128)}), f32[32,64,128]{2,1,0:T(8,128)}) %reduce-scatter.5.cloned.1.call-update) | async-done | bytes 1048592 | tf_op jit(solution)/shard_map/reduce_scatter | solution.py:81
  302.6 1.7 convert_reduce_fusion.2
  304.3 1.9 fusion.26
  306.2 0.7 fusion.34
  306.9 1.7 fusion.9
  (28 shorter events, 0.1 us)
Async XLA Ops:
  6.5 7.4 %copy-start.2 = (bf16[32,64,128]{2,1,0:T(8,128)(2,1)S(1)}, bf16[32,64,128]{2,1,0:T(8,128)(2,1)}, u32[]{:S(2)}) copy-start(bf16[32,64,128]{2,1,0:T(8,128)(2,1)} %param.10) | copy-start | bytes 1572868
  6.5 7.4 %copy-start.9 = (bf16[2,128,256]{2,1,0:T(8,128)(2,1)S(1)}, bf16[2,128,256]{2,1,0:T(8,128)(2,1)}, u32[]{:S(2)}) copy-start(bf16[2,128,256]{2,1,0:T(8,128)(2,1)} %param.15) | copy-start | bytes 393220
  6.5 49.1 %all-gather.3.cloned.1.call-start = ((), (), s32[]{:S(2)}) async-start(), calls=%async_computation.2 | async-start | bytes 4718592 | tf_op jit(solution)/shard_map/all_gather | solution.py:64
  16.2 143.1 %reduce-scatter.3.cloned.1.call-start = ((), (), s32[]{:S(2)}) async-start(), calls=%async_computation.3 | async-start | bytes 5242880 | tf_op jit(solution)/shard_map/reduce_scatter | solution.py:68
  82.8 0.7 copy-start.7
  82.8 0.7 copy-start.8
  82.8 81.1 %copy-start.6 = (bf16[2,128,128]{2,1,0:T(8,128)(2,1)S(1)}, bf16[2,128,128]{2,1,0:T(8,128)(2,1)}, u32[]{:S(2)}) copy-start(bf16[2,128,128]{2,1,0:T(8,128)(2,1)} %param.18) | copy-start | bytes 196612
  82.8 132.8 %all-gather.5.cloned.1.call-start = ((), (), s32[]{:S(2)}) async-start(), calls=%async_computation.4 | async-start | bytes 2621440 | tf_op jit(solution)/shard_map/all_gather | solution.py:77
  159.3 3.9 %copy-start = (f32[32,64,128]{2,0,1:T(8,128)S(1)}, f32[32,64,128]{2,0,1:T(8,128)}, u32[]{:S(2)}) copy-start(f32[32,64,128]{2,0,1:T(8,128)} %reduce-scatter.3.cloned.1.call-done) | copy-start | bytes 3145732
  161.1 3.0 copy-start.10
  164.2 1.9 copy-start.5
  165.4 2.6 copy-start.3
  169.1 133.5 %reduce-scatter.5.cloned.1.call-start = ((), (), s32[]{:S(2)}) async-start(), calls=%async_computation.5 | async-start | bytes 9437184 | tf_op jit(solution)/shard_map/reduce_scatter | solution.py:81
  232.4 74.5 %copy-start.4 = (bf16[32,64,128]{2,1,0:T(8,128)(2,1)S(1)}, bf16[32,64,128]{2,1,0:T(8,128)(2,1)}, u32[]{:S(2)}) copy-start(bf16[32,64,128]{2,1,0:T(8,128)(2,1)} %copy-done.3) | copy-start | bytes 1572868
  302.6 3.6 %copy-start.1 = (f32[32,64,128]{2,1,0:T(8,128)S(1)}, f32[32,64,128]{2,1,0:T(8,128)}, u32[]{:S(2)}) copy-start(f32[32,64,128]{2,1,0:T(8,128)} %reduce-scatter.5.cloned.1.call-done) | copy-start | bytes 3145732
Sparse Core Ops, SparseCore 0:
  16.4 39.2 all-gather.2
  82.9 76.3 reduce-scatter.2
  169.2 46.3 all-gather.4
  232.5 70.0 reduce-scatter.4
where the time goes:
time: 317 us; the launch traced here: 315 us
  waiting for transfers between devices  228 us (72%)
  local copies, waits for them, and re-layouts  38.2 us (12%)
  matrix products  21.6 us (7%)
  between operations  13.4 us (4%)
  other arithmetic  13.1 us (4%)
    reduce_scatter x1, waiting for transfers between devices, shards(): lax.psum_scatter(partial_value, 'col', scatter_dimension=1, tiled=True)  75.9 us
    reduce_scatter x1, waiting for transfers between devices, shards(): lax.psum_scatter(partial_value, 'row', scatter_dimension=0, tiled=True)  70.2 us
    all_gather x1, waiting for transfers between devices, shards(): left_cols = lax.all_gather(left_side, 'col', axis=1, tiled=True)  44.7 us
    all_gather x1, waiting for transfers between devices, shards(): right_rows = lax.all_gather(right_side, 'row', axis=0, tiled=True)  37.7 us
    all_gather x1, local copies, waits for them, and re-layouts, shards(): right_rows = lax.all_gather(right_side, 'row', axis=0, tiled=True)  12.9 us
    transpose x1, local copies, waits for them, and re-layouts, shards(): jnp.einsum('kih,kjh->ijh', left_cols, right_side, preferred_element_type=...  8.86 us
    dot_general x1, matrix products, shards(): jnp.einsum('ikh,jkh->ijh', left_side, right_rows, preferred_element_type=...  8.33 us
  transfers between devices with their start and end apart: 4, of which 4 were waited for; matrix products, arithmetic and copies ran while one was open for 1% of the time, Pallas kernels for 0%

commit v1 on v0

--- a/solution.py
+++ b/solution.py
@@ -1,14 +1,419 @@
+import functools
+
 import jax
 import jax.numpy as jnp
 from jax import lax
+from jax.experimental import pallas as pl
+from jax.experimental.pallas import tpu as pltpu
 from jax.sharding import PartitionSpec as P
+
+LANES = 128
+EPS = 1e-05
+NT = (((1,), (1,)), ((), ()))
+TN = (((0,), (0,)), ((), ()))
+
+
+def double_sigmoid(half_x):
+    return jnp.tanh(half_x) + 1.0
+
+
+PER = 8
+PAD = 1
+
+
+def normalize_down(x, gain_col, bias_col):
+    average = jnp.mean(x, axis=0, keepdims=True)
+    centred = x - average
+    variance = jnp.mean(centred * centred, axis=0, keepdims=True)
+    return centred * lax.rsqrt(variance + EPS) * gain_col + bias_col
+
+
+def column(row, width):
+    return jnp.broadcast_to(row, (width, row.shape[1])).T
+
+
+def group_at(slot, groups):
+    return lax.rem(slot + groups - lax.rem(lax.axis_index("col"), groups), groups)
+
+
+def load_down(z_ref, chunk, groups):
+    lane_rows = z_ref.shape[0] // groups
+    columns = [
+        jnp.concatenate(
+            [
+                z_ref[chunk * PER + q + lane_rows * group_at(slot, groups)]
+                for slot in range(groups)
+            ],
+            axis=0,
+        ).astype(jnp.float32).T
+        for q in range(PER)
+    ]
+    return jnp.concatenate(columns, axis=1)
+
+
+def halves_weights(proj_ref, gate_ref, layer):
+    half = jnp.asarray(0.5, jnp.bfloat16)
+    return (proj_ref[layer] * half).T, (gate_ref[layer] * half).T
+
+
+def project_chunk(chunk, normed, mask, weights, scratch):
+    normed = (normed * mask).astype(jnp.bfloat16)
+    projected = jnp.dot(weights[0], normed, preferred_element_type=jnp.float32)
+    gating = jnp.dot(weights[1], normed, preferred_element_type=jnp.float32)
+    halves = double_sigmoid(gating) * projected
+    rows = halves.shape[0]
+    for q in range(PER):
+        first = (chunk * PER + q) * (rows + PAD)
+        scratch[first : first + rows, :] = halves[:, q * LANES : (q + 1) * LANES]
+
+
+def spread_halves(scratch, halves_ref, devices):
+    count, slots, lane_rows, _ = halves_ref.shape
+    per_device = slots // 2
+    hidden = count * per_device
+    for d in devices:
+        for slot in range(slots):
+            h = (slot // per_device) * hidden + d * per_device + slot % per_device
+            rows = scratch[pl.ds(h, lane_rows, stride=2 * hidden + PAD), :]
+            halves_ref[d, slot] = rows.astype(jnp.bfloat16)
+
+
+def slots_kernel(cols, slots_ref):
+    slots_ref[...] = lax.broadcasted_iota(jnp.int32, slots_ref.shape, 1) // cols
+
+
+def first_kernel(
+    groups, slots_ref, z_ref, gain_ref, bias_ref, proj_ref, gate_ref, mask_row_ref,
+    halves_ref, mask_ref, mask_col_ref, scratch,
+):
+    rows, cols, _ = z_ref.shape
+    tokens = mask_row_ref.shape[1]
+    lane_rows = rows // groups
+
+    shift = lax.rem(tokens - lax.axis_index("col") * cols, tokens)
+    mask_row = mask_row_ref[...].astype(jnp.float32)
+    from_here = pltpu.roll(jnp.broadcast_to(mask_row, (8, tokens)), shift, 1)[:, :LANES]
+    col_mask = from_here
+    for slot in range(1, groups):
+        col_mask = jnp.where(
+            slots_ref[...] == slot, pltpu.roll(from_here, slot * cols, 1), col_mask
+        )
+    mask_col_ref[...] = column(mask_row, LANES)
+    first_row = lax.axis_index("row") * rows
+    for s in range(lane_rows):
+        row_mask = jnp.zeros((1, LANES), jnp.float32)
+        for slot in range(groups):
+            row = first_row + s + lane_rows * group_at(slot, groups)
+            row_mask = jnp.where(
+                slots_ref[0:1, :] == slot, mask_col_ref[pl.ds(row, 1), :], row_mask
+            )
+        lanes = slice((s % PER) * LANES, (s % PER + 1) * LANES)
+        mask_ref[s // PER, :, lanes] = row_mask * col_mask[0:1]
+
+    weights = halves_weights(proj_ref, gate_ref, 0)
+    gain_col = column(gain_ref[0:1, :], PER * LANES)
+    bias_col = column(bias_ref[0:1, :], PER * LANES)
+    for chunk in range(lane_rows // PER):
+        normed = normalize_down(load_down(z_ref, chunk, groups), gain_col, bias_col)
+        project_chunk(chunk, normed, mask_ref[chunk], weights, scratch)
+    spread_halves(scratch, halves_ref, range(halves_ref.shape[0]))
+
+
+def gate_chunk(weight, normed):
+    gating = jnp.dot(weight, normed.astype(jnp.bfloat16), preferred_element_type=jnp.float32)
+    return double_sigmoid(gating)
+
+
+def gate_weights(closer_ref, gain_ref, bias_ref, layer):
+    weight = (closer_ref[layer] * jnp.asarray(0.5, jnp.bfloat16)).T
+    gain_col = column(gain_ref[layer : layer + 1, :], PER * LANES)
+    bias_col = column(bias_ref[layer : layer + 1, :], PER * LANES)
+    return weight, gain_col, bias_col
+
+
+def prepare_kernel(
+    groups, z_ref, gain_ref, bias_ref, closer_ref, out_gain_ref, out_bias_ref, final_ref,
+    proj_ref, gate_ref, mask_ref,
+    z_down_ref, closing_ref, final_down_ref, weights_ref, rows_ref, mask_out_ref,
+):
+    mask_out_ref[...] = mask_ref[...]
+    half = jnp.asarray(0.5, jnp.bfloat16)
+    for layer in range(2):
+        final_down_ref[layer] = (final_ref[layer] * half).T
+    weights_ref[0], weights_ref[1] = halves_weights(proj_ref, gate_ref, 1)
+    rows = [
+        (out_gain_ref, 0), (out_bias_ref, 0), (gain_ref, 1), (bias_ref, 1), (out_gain_ref, 1),
+        (out_bias_ref, 1),
+    ]
+    for n, (ref, layer) in enumerate(rows):
+        rows_ref[n : n + 1, :] = ref[layer : layer + 1, :]
+    weight, gain_col, bias_col = gate_weights(closer_ref, gain_ref, bias_ref, 0)
+
+    def body(chunk, carry):
+        z = load_down(z_ref, chunk, groups)
+        z_down_ref[chunk] = z.astype(jnp.bfloat16)
+        closing_ref[chunk] = gate_chunk(weight, normalize_down(z, gain_col, bias_col)).astype(
+            jnp.bfloat16
+        )
+        return carry
+
+    lax.fori_loop(0, z_down_ref.shape[0], body, 0, unroll=2)
+
+
+def closing_kernel(z_down_ref, gain_ref, bias_ref, closer_ref, closing_ref):
+    weight, gain_col, bias_col = gate_weights(closer_ref, gain_ref, bias_ref, 1)
+
+    def body(chunk, carry):
+        z = z_down_ref[chunk].astype(jnp.float32)
+        closing_ref[chunk] = gate_chunk(weight, normalize_down(z, gain_col, bias_col)).astype(
+            jnp.bfloat16
+        )
+        return carry
+
+    lax.fori_loop(0, z_down_ref.shape[0], body, 0, unroll=2)
+
+
+def finish_chunk(chunk, lane_rows, sums_scratch, gain_col, bias_col, final, closing_ref, z_down_ref):
+    hidden = final.shape[1]
+    summed = jnp.concatenate(
+        [
+            sums_scratch[pl.ds(chunk * PER + q, hidden, stride=lane_rows + PAD), :]
+            for q in range(PER)
+        ],
+        axis=1,
+    )
+    lifted = normalize_down(summed, gain_col, bias_col).astype(jnp.bfloat16)
+    update = jnp.dot(final, lifted, preferred_element_type=jnp.float32)
+    return (z_down_ref[chunk].astype(jnp.float32) + closing_ref[chunk].astype(jnp.float32) * update).astype(
+        jnp.bfloat16
+    )
+
+
+def load_sums(sums_ref, scratch):
+    devices, per_device, lane_rows, _ = sums_ref.shape
+    for d in range(devices):
+        for slot in range(per_device):
+            first = (d * per_device + slot) * (lane_rows + PAD)
+            scratch[first : first + lane_rows, :] = sums_ref[d, slot].astype(jnp.float32)
+
+
+def middle_kernel(
+    z_down_ref, sums_ref, closing_ref, final_ref, weights_ref, rows_ref, mask_ref,
+    halves_ref, z_out_ref, sums_scratch, scratch,
+):
+    lane_rows = sums_ref.shape[2]
+    load_sums(sums_ref, sums_scratch)
+    final = final_ref[0]
+    weights = weights_ref[0], weights_ref[1]
+    out_gain_col, out_bias_col, gain_col, bias_col = [
+        column(rows_ref[n : n + 1, :], PER * LANES) for n in range(4)
+    ]
+    for chunk in range(lane_rows // PER):
+        z = finish_chunk(
+            chunk, lane_rows, sums_scratch, out_gain_col, out_bias_col, final, closing_ref,
+            z_down_ref,
+        )
+        z_out_ref[chunk] = z
+        normed = normalize_down(z.astype(jnp.float32), gain_col, bias_col)
+        project_chunk(chunk, normed, mask_ref[chunk], weights, scratch)
+    spread_halves(scratch, halves_ref, range(halves_ref.shape[0]))
+
+
+def finish_kernel(
+    groups, z_down_ref, sums_ref, closing_ref, final_ref, rows_ref, out_hbm, sums_scratch, out_ref, out_sems,
+):
+    lane_rows = sums_ref.shape[2]
+    cols = LANES // groups
+    load_sums(sums_ref, sums_scratch)
+    final = final_ref[1]
+    gain_col, bias_col = [column(rows_ref[n : n + 1, :], PER * LANES) for n in (4, 5)]
+    copies = []
+    for chunk in range(lane_rows // PER):
+        z = finish_chunk(
+            chunk, lane_rows, sums_scratch, gain_col, bias_col, final, closing_ref, z_down_ref
+        ).astype(jnp.float32)
+        parts = [
+            z[:, q * LANES : (q + 1) * LANES].T.astype(jnp.bfloat16) for q in range(PER)
+        ]
+        for slot in range(groups):
+            first = chunk * PER + lane_rows * group_at(slot, groups)
+            for q in range(PER):
+                out_ref[first + q] = parts[q][slot * cols : (slot + 1) * cols]
+            some = pl.ds(first, PER)
+            copy = pltpu.make_async_copy(
+                out_ref.at[some], out_hbm.at[some], out_sems.at[chunk, slot]
+            )
+            copy.start()
+            copies.append(copy)
+    for copy in copies:
+        copy.wait()
+
+
+def triangle_kernel(layer, groups, mesh_rows, mesh_cols, halves_ref, sums_ref, left, right):
+    per_device = sums_ref.shape[1]
+    lane_rows = sums_ref.shape[2]
+    cols = LANES // groups
+    lane_slot = lax.broadcasted_iota(jnp.int32, (1, LANES), 1) // cols
+
+    def pick(pieces):
+        out = pieces[0]
+        for n in range(1, groups):
+            out = jnp.where(lane_slot == n, pieces[n], out)
+        return out
+
+    def turned(value, slots):
+        places = slots * cols % LANES
+        return pltpu.roll(value, places, 1) if places else value
+
+    def assemble(slot, target):
+        for r in range(mesh_rows):
+            for t in range(mesh_cols // groups):
+                blocks = [
+                    halves_ref[r * mesh_cols + t * groups + u, slot] for u in range(groups)
+                ]
+                for g in range(groups):
+                    piece = turned(pick([blocks[(n - g) % groups] for n in range(groups)]), -g)
+                    first = (r * groups + g) * lane_rows
+                    target[first : first + lane_rows, t * LANES : (t + 1) * LANES] = piece
+
+    for q in range(per_device):
+        assemble(q, left.at[q])
+        assemble(per_device + q, right.at[q])
+        summed = lax.dot_general(
+            left[q], right[q], NT if layer == 0 else TN, preferred_element_type=jnp.float32
+        ).astype(jnp.bfloat16)
+        for r in range(mesh_rows):
+            for t in range(mesh_cols // groups):
+                blocks = [
+                    turned(
+                        summed[
+                            (r * groups + g) * lane_rows : (r * groups + g + 1) * lane_rows,
+                            t * LANES : (t + 1) * LANES,
+                        ],
+                        g,
+                    )
+                    for g in range(groups)
+                ]
+                for u in range(groups):
+                    piece = pick([blocks[(n - u) % groups] for n in range(groups)])
+                    sums_ref[r * mesh_cols + t * groups + u, q] = piece
+
+
+def vmem(count):
+    return [pl.BlockSpec(memory_space=pltpu.VMEM)] * count
+
+
+def by_channel(mesh_rows, mesh_cols, pair_map, token_mask, norm_gain, norm_bias, proj_weight,
+               gate_weight, out_gain, out_bias, final_weight, output_gate):
+    rows, cols, channels = pair_map.shape
+    hidden = proj_weight.shape[2] // 2
+    tokens = token_mask.shape[0]
+    devices = mesh_rows * mesh_cols
+    per_device = hidden // devices
+    groups = LANES // cols
+    lane_rows = rows // groups
+    chunks = lane_rows // PER
+    params = pltpu.CompilerParams(vmem_limit_bytes=40 * 1024 * 1024)
+    halves_type = jax.ShapeDtypeStruct((devices, 2 * per_device, lane_rows, LANES), jnp.bfloat16)
+    sums_type = jax.ShapeDtypeStruct((devices, per_device, lane_rows, LANES), jnp.bfloat16)
+    down_type = jax.ShapeDtypeStruct((chunks, channels, PER * LANES), jnp.bfloat16)
+    closing_type = down_type
+    mask_type = jax.ShapeDtypeStruct((chunks, 1, PER * LANES), jnp.float32)
+    halves_scratch = pltpu.VMEM((lane_rows * (2 * hidden + PAD), LANES), jnp.float32)
+    sums_scratch = pltpu.VMEM((hidden * (lane_rows + PAD), LANES), jnp.float32)
+    hbm = pl.BlockSpec(memory_space=pltpu.HBM)
+    closing_cost = pl.CostEstimate(
+        flops=2 * rows * cols * channels * channels,
+        bytes_accessed=8 * rows * cols * channels,
+        transcendentals=rows * cols * channels,
+    )
+
+    def exchange(value):
+        return lax.all_to_all(value, ("row", "col"), split_axis=0, concat_axis=0, tiled=True)
+
+    def triangle(layer, halves):
+        return pl.pallas_call(
+            functools.partial(triangle_kernel, layer, groups, mesh_rows, mesh_cols),
+            out_shape=sums_type,
+            in_specs=vmem(1),
+            out_specs=pl.BlockSpec(memory_space=pltpu.VMEM),
+            scratch_shapes=[pltpu.VMEM((per_device, tokens, tokens), jnp.bfloat16)] * 2,
+            compiler_params=params,
+        )(halves)
+
+    slots = pl.pallas_call(
+        functools.partial(slots_kernel, cols),
+        out_shape=jax.ShapeDtypeStruct((8, LANES), jnp.int32),
+        out_specs=pl.BlockSpec(memory_space=pltpu.VMEM),
+        compiler_params=params,
+        cost_estimate=pl.CostEstimate(
+            flops=10**9, bytes_accessed=8 * LANES * 4, transcendentals=0
+        ),
+    )()
+    halves, mask = pl.pallas_call(
+        functools.partial(first_kernel, groups),
+        out_shape=(halves_type, mask_type),
+        in_specs=vmem(7),
+        out_specs=tuple(vmem(2)),
+        scratch_shapes=[pltpu.VMEM((tokens, LANES), jnp.float32), halves_scratch],
+        compiler_params=params,
+    )(slots, pair_map, norm_gain, norm_bias, proj_weight, gate_weight,
+      token_mask.reshape(1, tokens))
+    arrived = exchange(halves)
+    z_down, closing, final_down, weights, table, mask = pl.pallas_call(
+        functools.partial(prepare_kernel, groups),
+        out_shape=(
+            down_type,
+            closing_type,
+            jax.ShapeDtypeStruct((2, channels, hidden), jnp.bfloat16),
+            jax.ShapeDtypeStruct((2, 2 * hidden, channels), jnp.bfloat16),
+            jax.ShapeDtypeStruct((8, channels), jnp.float32),
+            mask_type,
+        ),
+        in_specs=vmem(10),
+        out_specs=tuple(vmem(6)),
+        compiler_params=params,
+        cost_estimate=closing_cost,
+    )(pair_map, norm_gain, norm_bias, output_gate, out_gain, out_bias, final_weight, proj_weight,
+      gate_weight, mask)
+    sums = exchange(triangle(0, arrived))
+    halves, z_down = pl.pallas_call(
+        middle_kernel,
+        out_shape=(halves_type, down_type),
+        in_specs=vmem(7),
+        out_specs=tuple(vmem(2)),
+        scratch_shapes=[sums_scratch, halves_scratch],
+        compiler_params=params,
+    )(z_down, sums, closing, final_down, weights, table, mask)
+    arrived = exchange(halves)
+    closing = pl.pallas_call(
+        closing_kernel,
+        out_shape=closing_type,
+        in_specs=vmem(4),
+        out_specs=pl.BlockSpec(memory_space=pltpu.VMEM),
+        compiler_params=params,
+        cost_estimate=closing_cost,
+    )(z_down, norm_gain, norm_bias, output_gate)
+    sums = exchange(triangle(1, arrived))
+    return pl.pallas_call(
+        functools.partial(finish_kernel, groups),
+        out_shape=jax.ShapeDtypeStruct(pair_map.shape, jnp.bfloat16),
+        in_specs=vmem(5),
+        out_specs=hbm,
+        scratch_shapes=[
+            sums_scratch,
+            pltpu.VMEM(pair_map.shape, jnp.bfloat16),
+            pltpu.SemaphoreType.DMA((chunks, groups)),
+        ],
+        compiler_params=params,
+    )(z_down, sums, closing, final_down, table)
 
 
 def normalize(values, gain_vector, bias_vector):
     average = jnp.mean(values, axis=-1, keepdims=True)
     centred = values - average
     variance = jnp.mean(centred * centred, axis=-1, keepdims=True)
-    return centred * lax.rsqrt(variance + 1e-05) * gain_vector + bias_vector
+    return centred * lax.rsqrt(variance + EPS) * gain_vector + bias_vector
 
 
 def project(
@@ -34,18 +439,8 @@
     return (pair_map.astype(jnp.float32) + update).astype(jnp.bfloat16)
 
 
-def shards(
-    pair_map,
-    token_mask,
-    norm_gain,
-    norm_bias,
-    proj_weight,
-    gate_weight,
-    out_gain,
-    out_bias,
-    final_weight,
-    output_gate,
-):
+def by_block(pair_map, token_mask, norm_gain, norm_bias, proj_weight, gate_weight, out_gain,
+             out_bias, final_weight, output_gate):
     rows_here = pair_map.shape[0]
     cols_here = pair_map.shape[1]
     hidden = proj_weight.shape[2] // 2
@@ -85,6 +480,23 @@
 
 
 def solution(mesh):
+    mesh_rows, mesh_cols = mesh.shape["row"], mesh.shape["col"]
+
+    def shards(pair_map, token_mask, norm_gain, norm_bias, proj_weight, *rest):
+        rows, cols, _ = pair_map.shape
+        hidden = proj_weight.shape[2] // 2
+        groups = max(LANES // cols, 1)
+        fits = (
+            hidden % (mesh_rows * mesh_cols) == 0
+            and LANES % cols == 0
+            and rows % (16 * groups) == 0
+            and mesh_cols % groups == 0
+        )
+        args = (pair_map, token_mask, norm_gain, norm_bias, proj_weight, *rest)
+        if fits:
+            return by_channel(mesh_rows, mesh_cols, *args)
+        return by_block(*args)
+
     return jax.shard_map(
         shards,
         mesh=mesh,

time: 317 us -> 108 us (0.34)
  waiting for transfers between devices: 228 us -> 28.5 us
  blocking collectives: 0 us -> 62.6 us
  local copies, waits for them, and re-layouts: 38.2 us -> 1.8 us
  matrix products: 21.6 us -> 0 us
  between operations: 13.4 us -> 0.12 us
  other arithmetic: 13.1 us -> 0 us
  Pallas kernels: 0 us -> 8.57 us
  starting transfers between devices: 0.31 us -> 6.31 us
    reduce_scatter x2 -> x0, waiting for transfers between devices: 146 us -> none  [the longest x1 75.9 us: shards(): lax.psum_scatter(partial_value, 'col', scatter_dimension=1, tiled=True)]
    all_gather x2 -> x0, waiting for transfers between devices: 82.4 us -> none  [the longest x1 44.7 us: shards(): left_cols = lax.all_gather(left_side, 'col', axis=1, tiled=True)]
    all_to_all x0 -> x2, blocking collectives: none -> 62.6 us  [exchange(): lax.all_to_all(value, ('row', 'col'), split_axis=0, concat_axis=0, tiled=...]
    all_to_all x0 -> x2, waiting for transfers between devices: none -> 28.5 us  [exchange(): lax.all_to_all(value, ('row', 'col'), split_axis=0, concat_axis=0, tiled=...]
    dot_general x10 -> x0, matrix products: 21.6 us -> none  [the longest x1 8.33 us: shards(): jnp.einsum('ikh,jkh->ijh', left_side, right_rows, preferred_element_type=...]
    all_gather x2 -> x0, local copies, waits for them, and re-layouts: 16.3 us -> none  [the longest x1 12.9 us: shards(): right_rows = lax.all_gather(right_side, 'row', axis=0, tiled=True)]
    transpose x2 -> x0, local copies, waits for them, and re-layouts: 14.8 us -> none  [the longest x1 8.86 us: shards(): jnp.einsum('kih,kjh->ijh', left_cols, right_side, preferred_element_type=...]
    reduce_sum x7 -> x0, other arithmetic: 10.8 us -> none  [the longest x4 6.08 us: normalize(): variance = jnp.mean(centred * centred, axis=-1, keepdims=True)]
  transfers between devices with their start and end apart: 4 -> 2, of which waited for: 4 -> 2; matrix products, arithmetic and copies ran while one was open for 1% -> 0% of each run, Pallas kernels for 0% -> 1%
where the time goes in v1:
time: 108 us
  blocking collectives  62.6 us (58%)
  waiting for transfers between devices  28.5 us (26%)
  Pallas kernels  8.57 us (8%)
  starting transfers between devices  6.31 us (6%)
  local copies, waits for them, and re-layouts  1.8 us (2%)
    all_to_all x2, blocking collectives, exchange(): lax.all_to_all(value, ('row', 'col'), split_axis=0, concat_axis=0, tiled=...  62.6 us
    all_to_all x2, waiting for transfers between devices, exchange(): lax.all_to_all(value, ('row', 'col'), split_axis=0, concat_axis=0, tiled=...  28.5 us
    all_to_all x2, starting transfers between devices, exchange(): lax.all_to_all(value, ('row', 'col'), split_axis=0, concat_axis=0, tiled=...  6.31 us
    pallas_call x2, Pallas kernels, triangle(): pl.pallas_call(functools.partial(triangle_kernel, layer, groups, mesh_row...  2.83 us
  transfers between devices with their start and end apart: 2, of which 2 were waited for; matrix products, arithmetic and copies ran while one was open for 0% of the time, Pallas kernels for 1%

profile of v1, /device:TPU:1, one launch (start us, length us, event | category | flops | bytes accessed | tf_op | source)
XLA Modules:
  0.0 107.9 jit_solution(6425016089962170933)
XLA Ops:
  0.0 0.0 copy-start.2
  0.0 0.0 copy-start.1
  0.0 0.0 copy-start
  0.0 0.0 copy-start.6
  0.0 0.0 copy-start.7
  0.0 0.0 copy-start.5
  0.1 0.9 copy-done.2
  0.9 0.1 copy-done.1
  1.0 0.2 copy-done
  1.2 0.0 copy-done.6
  1.2 0.0 copy-done.7
  1.2 0.0 copy-done.5
  1.2 1.2 %shard_map.101 = (bf16[32,8,16,128]{3,2,1,0:T(8,128)(2,1)S(1)}, f32[2,1,1024]{2,1,0:T(1,128)S(1)}) custom-call(s32[8,128]{1,0:T(8,128)S(1)} %shard_map.100.slots_ref, bf16[32,64,128]{2,1,0:T(8,128)(2,1)S(1)} %copy-done, f32[2,128]{1,0:T(2,128)S(1)} %copy-done.5, f32[2,128]{1,0:T(2,128)S(1)} %copy-done.6, bf16[2,128,256]{2,1,0:T(8,128)(2,1)S(1)} %copy-done.1, ...), custom_call_target="tpu_custom_call" | custom-call | tf_op jit(solution)/shard_map/pallas_call | solution.py:353
  2.4 33.3 %all_to_all.20.halves_ref = bf16[32,8,16,128]{3,2,1,0:T(8,128)(2,1)S(1)} all-to-all(bf16[32,8,16,128]{3,2,1,0:T(8,128)(2,1)S(1)} %get-tuple-element.17), channel_id=1, replica_groups=mesh['row'=8,'col'=4] {'row','col'}, dimensions={0} | all-to-all | bytes 2097152 | tf_op jit(solution)/shard_map/all_to_all | solution.py:332
  35.6 1.3 %shard_map.103 = bf16[32,4,16,128]{3,2,1,0:T(8,128)(2,1)} custom-call(bf16[32,8,16,128]{3,2,1,0:T(8,128)(2,1)S(1)} %all_to_all.20.halves_ref), custom_call_target="tpu_custom_call" | custom-call | tf_op jit(solution)/shard_map/pallas_call | solution.py:335
  37.0 0.0 copy-start.3
  37.0 0.0 copy-start.4
  37.0 0.0 copy-start.9
  37.0 3.2 %all-to-all-start.1 = ((bf16[32,4,16,128]{3,2,1,0:T(8,128)(2,1)}), bf16[32,4,16,128]{3,2,1,0:T(8,128)(2,1)S(1)}, u32[]{:S(2)}, u32[]{:S(2)}) async-start(bf16[32,4,16,128]{3,2,1,0:T(8,128)(2,1)} %shard_map.103), calls=%async_computation.1 | async-start | bytes 1048576 | tf_op jit(solution)/shard_map/all_to_all | solution.py:332
  40.1 0.0 copy-start.8
  40.1 0.0 copy-done.3
  40.2 0.0 copy-done.4
  40.2 0.0 copy-done.9
  40.2 0.6 copy-done.8
  40.8 0.8 shard_map.102
  41.6 13.9 %all-to-all-done.1.sums_ref = bf16[32,4,16,128]{3,2,1,0:T(8,128)(2,1)S(1)} async-done(((bf16[32,4,16,128]{3,2,1,0:T(8,128)(2,1)}), bf16[32,4,16,128]{3,2,1,0:T(8,128)(2,1)S(1)}, u32[]{:S(2)}, u32[]{:S(2)}) %all-to-all-start.1) | async-done | bytes 524320 | tf_op jit(solution)/shard_map/all_to_all | solution.py:332
  55.4 1.7 %shard_map.104 = (bf16[32,8,16,128]{3,2,1,0:T(8,128)(2,1)S(1)}, bf16[2,128,1024]{2,1,0:T(8,128)(2,1)S(1)}) custom-call(bf16[2,128,1024]{2,1,0:T(8,128)(2,1)S(1)} %get-tuple-element.16.z_down_ref, bf16[32,4,16,128]{3,2,1,0:T(8,128)(2,1)S(1)} %all-to-all-done.1.sums_ref, bf16[2,128,1024]{2,1,0:T(8,128)(2,1)S(1)} %get-tuple-element.18.closing_ref, ...), custom_call_target="tpu_custom_call" | custom-call | tf_op jit(solution)/shard_map/pallas_call | solution.py:380
  57.2 29.3 %all_to_all.21.halves_ref = bf16[32,8,16,128]{3,2,1,0:T(8,128)(2,1)S(1)} all-to-all(bf16[32,8,16,128]{3,2,1,0:T(8,128)(2,1)S(1)} %get-tuple-element.24), channel_id=1, replica_groups=mesh['row'=8,'col'=4] {'row','col'}, dimensions={0} | all-to-all | bytes 2097152 | tf_op jit(solution)/shard_map/all_to_all | solution.py:332
  86.5 1.5 %shard_map.105 = bf16[32,4,16,128]{3,2,1,0:T(8,128)(2,1)} custom-call(bf16[32,8,16,128]{3,2,1,0:T(8,128)(2,1)S(1)} %all_to_all.21.halves_ref), custom_call_target="tpu_custom_call" | custom-call | tf_op jit(solution)/shard_map/pallas_call | solution.py:335
  88.0 3.2 %all-to-all-start.3 = ((bf16[32,4,16,128]{3,2,1,0:T(8,128)(2,1)}), bf16[32,4,16,128]{3,2,1,0:T(8,128)(2,1)S(1)}, u32[]{:S(2)}, u32[]{:S(2)}) async-start(bf16[32,4,16,128]{3,2,1,0:T(8,128)(2,1)} %shard_map.105), calls=%async_computation.3 | async-start | bytes 1048576 | tf_op jit(solution)/shard_map/all_to_all | solution.py:332
  91.2 0.6 shard_map.106.closing_ref
  91.8 14.7 %all-to-all-done.3.sums_ref = bf16[32,4,16,128]{3,2,1,0:T(8,128)(2,1)S(1)} async-done(((bf16[32,4,16,128]{3,2,1,0:T(8,128)(2,1)}), bf16[32,4,16,128]{3,2,1,0:T(8,128)(2,1)S(1)}, u32[]{:S(2)}, u32[]{:S(2)}) %all-to-all-start.3) | async-done | bytes 524320 | tf_op jit(solution)/shard_map/all_to_all | solution.py:332
  106.4 1.5 %shard_map.107 = bf16[32,64,128]{2,1,0:T(8,128)(2,1)} custom-call(bf16[2,128,1024]{2,1,0:T(8,128)(2,1)S(1)} %get-tuple-element.23.z_down_ref, bf16[32,4,16,128]{3,2,1,0:T(8,128)(2,1)S(1)} %all-to-all-done.3.sums_ref, bf16[2,128,1024]{2,1,0:T(8,128)(2,1)S(1)} %shard_map.106.closing_ref, bf16[2,128,128]{2,1,0:T(8,128)(2,1)S(1)} %get-tuple-element.19.final_ref, ...), custom_call_target="tpu_custom_call" | custom-call | tf_op jit(solution)/shard_map/pallas_call | solution.py:398
  (1 shorter events, 0.0 us)
Async XLA Ops:
  0.0 0.9 copy-start.2
  0.0 1.0 copy-start.1
  0.0 1.2 %copy-start = (bf16[32,64,128]{2,1,0:T(8,128)(2,1)S(1)}, bf16[32,64,128]{2,1,0:T(8,128)(2,1)}, u32[]{:S(2)}) copy-start(bf16[32,64,128]{2,1,0:T(8,128)(2,1)} %z_ref.3) | copy-start | bytes 1572868
  0.0 1.2 %copy-start.6 = (f32[2,128]{1,0:T(2,128)S(1)}, f32[2,128]{1,0:T(2,128)}, u32[]{:S(2)}) copy-start(f32[2,128]{1,0:T(2,128)} %bias_ref.5) | copy-start | bytes 3076
  0.0 1.2 %copy-start.7 = (s32[256]{0:T(256)S(1)}, s32[256]{0:T(256)}, u32[]{:S(2)}) copy-start(s32[256]{0:T(256)} %param.11) | copy-start | bytes 3076
  0.0 1.1 %copy-start.5 = (f32[2,128]{1,0:T(2,128)S(1)}, f32[2,128]{1,0:T(2,128)}, u32[]{:S(2)}) copy-start(f32[2,128]{1,0:T(2,128)} %gain_ref.5) | copy-start | bytes 3076
  37.0 3.2 %copy-start.3 = (bf16[2,128,128]{2,1,0:T(8,128)(2,1)S(1)}, bf16[2,128,128]{2,1,0:T(8,128)(2,1)}, u32[]{:S(2)}) copy-start(bf16[2,128,128]{2,1,0:T(8,128)(2,1)} %closer_ref.3) | copy-start | bytes 196612
  37.0 3.2 %copy-start.4 = (bf16[2,128,128]{2,1,0:T(8,128)(2,1)S(1)}, bf16[2,128,128]{2,1,0:T(8,128)(2,1)}, u32[]{:S(2)}) copy-start(bf16[2,128,128]{2,1,0:T(8,128)(2,1)} %final_ref.1) | copy-start | bytes 196612
  37.0 3.2 %copy-start.9 = (f32[2,128]{1,0:T(2,128)S(1)}, f32[2,128]{1,0:T(2,128)}, u32[]{:S(2)}) copy-start(f32[2,128]{1,0:T(2,128)} %out_bias_ref.1) | copy-start | bytes 3076
  37.0 18.5 %all-to-all-start.1 = ((bf16[32,4,16,128]{3,2,1,0:T(8,128)(2,1)}), bf16[32,4,16,128]{3,2,1,0:T(8,128)(2,1)S(1)}, u32[]{:S(2)}, u32[]{:S(2)}) async-start(bf16[32,4,16,128]{3,2,1,0:T(8,128)(2,1)} %shard_map.103), calls=%async_computation.1 | async-start | bytes 1048576 | tf_op jit(solution)/shard_map/all_to_all | solution.py:332
  40.1 0.7 copy-start.8
  88.0 18.5 %all-to-all-start.3 = ((bf16[32,4,16,128]{3,2,1,0:T(8,128)(2,1)}), bf16[32,4,16,128]{3,2,1,0:T(8,128)(2,1)S(1)}, u32[]{:S(2)}, u32[]{:S(2)}) async-start(bf16[32,4,16,128]{3,2,1,0:T(8,128)(2,1)} %shard_map.105), calls=%async_computation.3 | async-start | bytes 1048576 | tf_op jit(solution)/shard_map/all_to_all | solution.py:332

commit v2 on v1

--- a/solution.py
+++ b/solution.py
@@ -17,7 +17,7 @@
     return jnp.tanh(half_x) + 1.0
 
 
-PER = 8
+PER = 16
 PAD = 1
 
 
@@ -83,8 +83,10 @@
 
 
 def first_kernel(
-    groups, slots_ref, z_ref, gain_ref, bias_ref, proj_ref, gate_ref, mask_row_ref,
-    halves_ref, mask_ref, mask_col_ref, scratch,
+    groups, slots_ref, z_ref, gain_ref, bias_ref, proj_ref, gate_ref, mask_row_ref, closer_ref,
+    out_gain_ref, out_bias_ref, final_ref,
+    halves_ref, mask_ref, z_down_ref, closing_ref, turned_ref, weights_ref, rows_ref,
+    mask_col_ref, scratch,
 ):
     rows, cols, _ = z_ref.shape
     tokens = mask_row_ref.shape[1]
@@ -110,67 +112,34 @@
         lanes = slice((s % PER) * LANES, (s % PER + 1) * LANES)
         mask_ref[s // PER, :, lanes] = row_mask * col_mask[0:1]
 
+    half = jnp.asarray(0.5, jnp.bfloat16)
+    turned_ref[0] = (final_ref[0] * half).T
+    turned_ref[1] = (closer_ref[1] * half).T
+    turned_ref[2] = (final_ref[1] * half).T
+    weights_ref[0], weights_ref[1] = halves_weights(proj_ref, gate_ref, 1)
+    table = [
+        (out_gain_ref, 0), (out_bias_ref, 0), (gain_ref, 1), (bias_ref, 1), (out_gain_ref, 1),
+        (out_bias_ref, 1),
+    ]
+    for n, (ref, layer) in enumerate(table):
+        rows_ref[n : n + 1, :] = ref[layer : layer + 1, :]
+
     weights = halves_weights(proj_ref, gate_ref, 0)
+    closer = (closer_ref[0] * half).T
     gain_col = column(gain_ref[0:1, :], PER * LANES)
     bias_col = column(bias_ref[0:1, :], PER * LANES)
     for chunk in range(lane_rows // PER):
-        normed = normalize_down(load_down(z_ref, chunk, groups), gain_col, bias_col)
+        z = load_down(z_ref, chunk, groups)
+        z_down_ref[chunk] = z.astype(jnp.bfloat16)
+        normed = normalize_down(z, gain_col, bias_col)
+        closing_ref[chunk] = gate_chunk(closer, normed)
         project_chunk(chunk, normed, mask_ref[chunk], weights, scratch)
     spread_halves(scratch, halves_ref, range(halves_ref.shape[0]))
 
 
 def gate_chunk(weight, normed):
     gating = jnp.dot(weight, normed.astype(jnp.bfloat16), preferred_element_type=jnp.float32)
-    return double_sigmoid(gating)
-
-
-def gate_weights(closer_ref, gain_ref, bias_ref, layer):
-    weight = (closer_ref[layer] * jnp.asarray(0.5, jnp.bfloat16)).T
-    gain_col = column(gain_ref[layer : layer + 1, :], PER * LANES)
-    bias_col = column(bias_ref[layer : layer + 1, :], PER * LANES)
-    return weight, gain_col, bias_col
-
-
-def prepare_kernel(
-    groups, z_ref, gain_ref, bias_ref, closer_ref, out_gain_ref, out_bias_ref, final_ref,
-    proj_ref, gate_ref, mask_ref,
-    z_down_ref, closing_ref, final_down_ref, weights_ref, rows_ref, mask_out_ref,
-):
-    mask_out_ref[...] = mask_ref[...]
-    half = jnp.asarray(0.5, jnp.bfloat16)
-    for layer in range(2):
-        final_down_ref[layer] = (final_ref[layer] * half).T
-    weights_ref[0], weights_ref[1] = halves_weights(proj_ref, gate_ref, 1)
-    rows = [
-        (out_gain_ref, 0), (out_bias_ref, 0), (gain_ref, 1), (bias_ref, 1), (out_gain_ref, 1),
-        (out_bias_ref, 1),
-    ]
-    for n, (ref, layer) in enumerate(rows):
-        rows_ref[n : n + 1, :] = ref[layer : layer + 1, :]
-    weight, gain_col, bias_col = gate_weights(closer_ref, gain_ref, bias_ref, 0)
-
-    def body(chunk, carry):
-        z = load_down(z_ref, chunk, groups)
-        z_down_ref[chunk] = z.astype(jnp.bfloat16)
-        closing_ref[chunk] = gate_chunk(weight, normalize_down(z, gain_col, bias_col)).astype(
-            jnp.bfloat16
-        )
-        return carry
-
-    lax.fori_loop(0, z_down_ref.shape[0], body, 0, unroll=2)
-
-
-def closing_kernel(z_down_ref, gain_ref, bias_ref, closer_ref, closing_ref):
-    weight, gain_col, bias_col = gate_weights(closer_ref, gain_ref, bias_ref, 1)
-
-    def body(chunk, carry):
-        z = z_down_ref[chunk].astype(jnp.float32)
-        closing_ref[chunk] = gate_chunk(weight, normalize_down(z, gain_col, bias_col)).astype(
-            jnp.bfloat16
-        )
-        return carry
-
-    lax.fori_loop(0, z_down_ref.shape[0], body, 0, unroll=2)
+    return double_sigmoid(gating).astype(jnp.bfloat16)
 
 
 def finish_chunk(chunk, lane_rows, sums_scratch, gain_col, bias_col, final, closing_ref, z_down_ref):
@@ -198,12 +167,12 @@
 
 
 def middle_kernel(
-    z_down_ref, sums_ref, closing_ref, final_ref, weights_ref, rows_ref, mask_ref,
-    halves_ref, z_out_ref, sums_scratch, scratch,
+    z_down_ref, sums_ref, closing_ref, turned_ref, weights_ref, rows_ref, mask_ref,
+    halves_ref, z_out_ref, closing_out_ref, sums_scratch, scratch,
 ):
     lane_rows = sums_ref.shape[2]
     load_sums(sums_ref, sums_scratch)
-    final = final_ref[0]
+    final, closer = turned_ref[0], turned_ref[1]
     weights = weights_ref[0], weights_ref[1]
     out_gain_col, out_bias_col, gain_col, bias_col = [
         column(rows_ref[n : n + 1, :], PER * LANES) for n in range(4)
@@ -215,41 +184,46 @@
         )
         z_out_ref[chunk] = z
         normed = normalize_down(z.astype(jnp.float32), gain_col, bias_col)
+        closing_out_ref[chunk] = gate_chunk(closer, normed)
         project_chunk(chunk, normed, mask_ref[chunk], weights, scratch)
     spread_halves(scratch, halves_ref, range(halves_ref.shape[0]))
 
 
 def finish_kernel(
-    groups, z_down_ref, sums_ref, closing_ref, final_ref, rows_ref, out_hbm, sums_scratch, out_ref, out_sems,
+    groups, z_down_ref, sums_ref, closing_ref, turned_ref, rows_ref, out_hbm, sums_scratch, out_ref, out_sems,
 ):
     lane_rows = sums_ref.shape[2]
     cols = LANES // groups
     load_sums(sums_ref, sums_scratch)
-    final = final_ref[1]
+    final = turned_ref[2]
     gain_col, bias_col = [column(rows_ref[n : n + 1, :], PER * LANES) for n in (4, 5)]
     copies = []
     for chunk in range(lane_rows // PER):
         z = finish_chunk(
             chunk, lane_rows, sums_scratch, gain_col, bias_col, final, closing_ref, z_down_ref
         ).astype(jnp.float32)
-        parts = [
-            z[:, q * LANES : (q + 1) * LANES].T.astype(jnp.bfloat16) for q in range(PER)
-        ]
-        for slot in range(groups):
-            first = chunk * PER + lane_rows * group_at(slot, groups)
-            for q in range(PER):
-                out_ref[first + q] = parts[q][slot * cols : (slot + 1) * cols]
-            some = pl.ds(first, PER)
-            copy = pltpu.make_async_copy(
-                out_ref.at[some], out_hbm.at[some], out_sems.at[chunk, slot]
-            )
-            copy.start()
-            copies.append(copy)
+        half = PER // 2
+        for first_q in range(0, PER, half):
+            for q in range(first_q, first_q + half):
+                part = z[:, q * LANES : (q + 1) * LANES].T.astype(jnp.bfloat16)
+                for slot in range(groups):
+                    row = chunk * PER + q + lane_rows * group_at(slot, groups)
+                    out_ref[row] = part[slot * cols : (slot + 1) * cols]
+            for slot in range(groups):
+                row = chunk * PER + first_q + lane_rows * group_at(slot, groups)
+                some = pl.ds(row, half)
+                copy = pltpu.make_async_copy(
+                    out_ref.at[some], out_hbm.at[some], out_sems.at[len(copies)]
+                )
+                copy.start()
+                copies.append(copy)
     for copy in copies:
         copy.wait()
 
 
-def triangle_kernel(layer, groups, mesh_rows, mesh_cols, halves_ref, sums_ref, left, right):
+def triangle_kernel(
+    layer, groups, mesh_rows, mesh_cols, halves_ref, sums_ref, left, right
+):
     per_device = sums_ref.shape[1]
     lane_rows = sums_ref.shape[2]
     cols = LANES // groups
@@ -317,17 +291,10 @@
     halves_type = jax.ShapeDtypeStruct((devices, 2 * per_device, lane_rows, LANES), jnp.bfloat16)
     sums_type = jax.ShapeDtypeStruct((devices, per_device, lane_rows, LANES), jnp.bfloat16)
     down_type = jax.ShapeDtypeStruct((chunks, channels, PER * LANES), jnp.bfloat16)
-    closing_type = down_type
     mask_type = jax.ShapeDtypeStruct((chunks, 1, PER * LANES), jnp.float32)
-    halves_scratch = pltpu.VMEM((lane_rows * (2 * hidden + PAD), LANES), jnp.float32)
-    sums_scratch = pltpu.VMEM((hidden * (lane_rows + PAD), LANES), jnp.float32)
+    halves_scratch = pltpu.VMEM(((lane_rows + 1) * (2 * hidden + PAD), LANES), jnp.float32)
+    sums_scratch = pltpu.VMEM(((hidden + 1) * (lane_rows + PAD), LANES), jnp.float32)
     hbm = pl.BlockSpec(memory_space=pltpu.HBM)
-    closing_cost = pl.CostEstimate(
-        flops=2 * rows * cols * channels * channels,
-        bytes_accessed=8 * rows * cols * channels,
-        transcendentals=rows * cols * channels,
-    )
-
     def exchange(value):
         return lax.all_to_all(value, ("row", "col"), split_axis=0, concat_axis=0, tiled=True)
 
@@ -350,51 +317,33 @@
             flops=10**9, bytes_accessed=8 * LANES * 4, transcendentals=0
         ),
     )()
-    halves, mask = pl.pallas_call(
+    halves, mask, z_down, closing, turned, weights, table = pl.pallas_call(
         functools.partial(first_kernel, groups),
-        out_shape=(halves_type, mask_type),
-        in_specs=vmem(7),
-        out_specs=tuple(vmem(2)),
+        out_shape=(
+            halves_type,
+            mask_type,
+            down_type,
+            down_type,
+            jax.ShapeDtypeStruct((3, channels, hidden), jnp.bfloat16),
+            jax.ShapeDtypeStruct((2, 2 * hidden, channels), jnp.bfloat16),
+            jax.ShapeDtypeStruct((8, channels), jnp.float32),
+        ),
+        in_specs=vmem(11),
+        out_specs=tuple(vmem(7)),
         scratch_shapes=[pltpu.VMEM((tokens, LANES), jnp.float32), halves_scratch],
         compiler_params=params,
     )(slots, pair_map, norm_gain, norm_bias, proj_weight, gate_weight,
-      token_mask.reshape(1, tokens))
-    arrived = exchange(halves)
-    z_down, closing, final_down, weights, table, mask = pl.pallas_call(
-        functools.partial(prepare_kernel, groups),
-        out_shape=(
-            down_type,
-            closing_type,
-            jax.ShapeDtypeStruct((2, channels, hidden), jnp.bfloat16),
-            jax.ShapeDtypeStruct((2, 2 * hidden, channels), jnp.bfloat16),
-            jax.ShapeDtypeStruct((8, channels), jnp.float32),
-            mask_type,
-        ),
-        in_specs=vmem(10),
-        out_specs=tuple(vmem(6)),
-        compiler_params=params,
-        cost_estimate=closing_cost,
-    )(pair_map, norm_gain, norm_bias, output_gate, out_gain, out_bias, final_weight, proj_weight,
-      gate_weight, mask)
-    sums = exchange(triangle(0, arrived))
-    halves, z_down = pl.pallas_call(
+      token_mask.reshape(1, tokens), output_gate, out_gain, out_bias, final_weight)
+    sums = exchange(triangle(0, exchange(halves)))
+    halves, z_down, closing = pl.pallas_call(
         middle_kernel,
-        out_shape=(halves_type, down_type),
+        out_shape=(halves_type, down_type, down_type),
         in_specs=vmem(7),
-        out_specs=tuple(vmem(2)),
+        out_specs=tuple(vmem(3)),
         scratch_shapes=[sums_scratch, halves_scratch],
         compiler_params=params,
-    )(z_down, sums, closing, final_down, weights, table, mask)
-    arrived = exchange(halves)
-    closing = pl.pallas_call(
-        closing_kernel,
-        out_shape=closing_type,
-        in_specs=vmem(4),
-        out_specs=pl.BlockSpec(memory_space=pltpu.VMEM),
-        compiler_params=params,
-        cost_estimate=closing_cost,
-    )(z_down, norm_gain, norm_bias, output_gate)
-    sums = exchange(triangle(1, arrived))
+    )(z_down, sums, closing, turned, weights, table, mask)
+    sums = exchange(triangle(1, exchange(halves)))
     return pl.pallas_call(
         functools.partial(finish_kernel, groups),
         out_shape=jax.ShapeDtypeStruct(pair_map.shape, jnp.bfloat16),
@@ -403,10 +352,10 @@
         scratch_shapes=[
             sums_scratch,
             pltpu.VMEM(pair_map.shape, jnp.bfloat16),
-            pltpu.SemaphoreType.DMA((chunks, groups)),
+            pltpu.SemaphoreType.DMA((2 * chunks * groups,)),
         ],
         compiler_params=params,
-    )(z_down, sums, closing, final_down, table)
+    )(z_down, sums, closing, turned, table)
 
 
 def normalize(values, gain_vector, bias_vector):

time: 108 us -> 107 us (level)
  blocking collectives: 62.6 us -> 99.1 us
  waiting for transfers between devices: 28.5 us -> 0 us
  starting transfers between devices: 6.31 us -> 0 us
  Pallas kernels: 8.57 us -> 6.22 us
    all_to_all x2 -> x4, blocking collectives: 62.6 us -> 99.1 us  [exchange(): lax.all_to_all(value, ('row', 'col'), split_axis=0, concat_axis=0, tiled=...]
    all_to_all x2 -> x0, waiting for transfers between devices: 28.5 us -> none  [exchange(): lax.all_to_all(value, ('row', 'col'), split_axis=0, concat_axis=0, tiled=...]
    all_to_all x2 -> x0, starting transfers between devices: 6.31 us -> none  [exchange(): lax.all_to_all(value, ('row', 'col'), split_axis=0, concat_axis=0, tiled=...]
    pallas_call x2, Pallas kernels: 2.83 us -> 1.23 us  [triangle(): pl.pallas_call(functools.partial(triangle_kernel, layer, groups, mesh_row...]
    pallas_call x3 -> x1, Pallas kernels: 3.1 us -> 1.95 us  [by_channel(): pl.pallas_call(middle_kernel, out_shape=(halves_type, down_type, down_typ...]
  transfers between devices with their start and end apart: 2 -> 0, of which waited for: 2 -> 0; matrix products, arithmetic and copies ran while one was open for 0% -> 0% of each run, Pallas kernels for 1% -> 0%
where the time goes in v2:
time: 107 us
  blocking collectives  99.1 us (93%)
  Pallas kernels  6.22 us (6%)
  local copies, waits for them, and re-layouts  1.18 us (1%)
    all_to_all x4, blocking collectives, exchange(): lax.all_to_all(value, ('row', 'col'), split_axis=0, concat_axis=0, tiled=...  99.1 us

profile of v2, /device:TPU:1, one launch (start us, length us, event | category | flops | bytes accessed | tf_op | source)
XLA Modules:
  0.0 106.6 jit_solution(4996144563328749366)
XLA Ops:
  0.0 0.0 copy-start.3
  0.0 0.0 copy-start.4
  0.0 0.0 copy-start.2
  0.0 0.0 copy-start.1
  0.0 0.0 copy-start
  0.0 0.0 copy-start.6
  0.0 0.0 copy-start.7
  0.0 0.0 copy-start.8
  0.1 0.0 copy-start.9
  0.1 0.0 copy-start.5
  0.1 0.7 copy-done.3
  0.8 0.0 copy-done.4
  0.9 0.1 copy-done.2
  1.0 0.1 copy-done.1
  1.0 0.2 copy-done
  1.2 0.0 copy-done.6
  1.2 0.0 copy-done.7
  1.3 0.0 copy-done.8
  1.3 0.0 copy-done.9
  1.3 0.0 copy-done.5
  1.3 1.5 %shard_map.101 = (bf16[32,8,16,128]{3,2,1,0:T(8,128)(2,1)S(1)}, f32[1,1,2048]{2,1,0:T(1,128)S(1)}, bf16[1,128,2048]{2,1,0:T(8,128)(2,1)S(1)}, bf16[1,128,2048]{2...) custom-call(s32[8,128]{1,0:T(8,128)S(1)} %shard_map.100.slots_ref, ...), custom_call_target="tpu_custom_call" | custom-call | tf_op jit(solution)/shard_map/pallas_call | solution.py:320
  2.8 33.3 %all_to_all.20.halves_ref = bf16[32,8,16,128]{3,2,1,0:T(8,128)(2,1)S(1)} all-to-all(bf16[32,8,16,128]{3,2,1,0:T(8,128)(2,1)S(1)} %get-tuple-element.16), channel_id=1, replica_groups=mesh['row'=8,'col'=4] {'row','col'}, dimensions={0} | all-to-all | bytes 2097152 | tf_op jit(solution)/shard_map/all_to_all | solution.py:299
  36.1 0.5 shard_map.102
  36.6 18.3 %all_to_all.21.sums_ref = bf16[32,4,16,128]{3,2,1,0:T(8,128)(2,1)S(1)} all-to-all(bf16[32,4,16,128]{3,2,1,0:T(8,128)(2,1)S(1)} %shard_map.102), channel_id=1, replica_groups=mesh['row'=8,'col'=4] {'row','col'}, dimensions={0} | all-to-all | bytes 1048576 | tf_op jit(solution)/shard_map/all_to_all | solution.py:299
  54.9 1.9 %shard_map.103 = (bf16[32,8,16,128]{3,2,1,0:T(8,128)(2,1)S(1)}, bf16[1,128,2048]{2,1,0:T(8,128)(2,1)S(1)}, bf16[1,128,2048]{2,1,0:T(8,128)(2,1)S(1)}) custom-call(bf16[1,128,2048]{2,1,0:T(8,128)(2,1)S(1)} %get-tuple-element.15.z_down_ref, bf16[32,4,16,128]{3,2,1,0:T(8,128)(2,1)S(1)} %all_to_all.21.sums_ref, ...), custom_call_target="tpu_custom_call" | custom-call | tf_op jit(solution)/shard_map/pallas_call | solution.py:338
  56.8 29.3 %all_to_all.22.halves_ref = bf16[32,8,16,128]{3,2,1,0:T(8,128)(2,1)S(1)} all-to-all(bf16[32,8,16,128]{3,2,1,0:T(8,128)(2,1)S(1)} %get-tuple-element.23), channel_id=1, replica_groups=mesh['row'=8,'col'=4] {'row','col'}, dimensions={0} | all-to-all | bytes 2097152 | tf_op jit(solution)/shard_map/all_to_all | solution.py:299
  86.1 0.7 shard_map.104
  86.8 18.3 %all_to_all.23.sums_ref = bf16[32,4,16,128]{3,2,1,0:T(8,128)(2,1)S(1)} all-to-all(bf16[32,4,16,128]{3,2,1,0:T(8,128)(2,1)S(1)} %shard_map.104), channel_id=1, replica_groups=mesh['row'=8,'col'=4] {'row','col'}, dimensions={0} | all-to-all | bytes 1048576 | tf_op jit(solution)/shard_map/all_to_all | solution.py:299
  105.1 1.5 %shard_map.105 = bf16[32,64,128]{2,1,0:T(8,128)(2,1)} custom-call(bf16[1,128,2048]{2,1,0:T(8,128)(2,1)S(1)} %get-tuple-element.22.z_down_ref, bf16[32,4,16,128]{3,2,1,0:T(8,128)(2,1)S(1)} %all_to_all.23.sums_ref, bf16[1,128,2048]{2,1,0:T(8,128)(2,1)S(1)} %get-tuple-element.24.closing_ref, bf16[3,128,128]{2,1,0:T(8,128)(2,1)S(1)} %get-tuple-element.18.turned_ref, ...), custom_call_target="tpu_custom_call" | custom-call | tf_op jit(solution)/shard_map/pallas_call | solution.py:347
  (1 shorter events, 0.0 us)
Async XLA Ops:
  0.0 0.8 copy-start.3
  0.0 0.9 copy-start.4
  0.0 1.0 copy-start.2
  0.0 1.0 copy-start.1
  0.0 1.2 %copy-start = (bf16[32,64,128]{2,1,0:T(8,128)(2,1)S(1)}, bf16[32,64,128]{2,1,0:T(8,128)(2,1)}, u32[]{:S(2)}) copy-start(bf16[32,64,128]{2,1,0:T(8,128)(2,1)} %z_ref.1) | copy-start | bytes 1572868
  0.0 1.2 %copy-start.6 = (f32[2,128]{1,0:T(2,128)S(1)}, f32[2,128]{1,0:T(2,128)}, u32[]{:S(2)}) copy-start(f32[2,128]{1,0:T(2,128)} %bias_ref.1) | copy-start | bytes 3076
  0.0 1.2 %copy-start.7 = (s32[256]{0:T(256)S(1)}, s32[256]{0:T(256)}, u32[]{:S(2)}) copy-start(s32[256]{0:T(256)} %param.11) | copy-start | bytes 3076
  0.0 1.2 %copy-start.8 = (f32[2,128]{1,0:T(2,128)S(1)}, f32[2,128]{1,0:T(2,128)}, u32[]{:S(2)}) copy-start(f32[2,128]{1,0:T(2,128)} %out_gain_ref.1) | copy-start | bytes 3076
  0.1 1.2 %copy-start.9 = (f32[2,128]{1,0:T(2,128)S(1)}, f32[2,128]{1,0:T(2,128)}, u32[]{:S(2)}) copy-start(f32[2,128]{1,0:T(2,128)} %out_bias_ref.1) | copy-start | bytes 3076
  0.1 1.2 %copy-start.5 = (f32[2,128]{1,0:T(2,128)S(1)}, f32[2,128]{1,0:T(2,128)}, u32[]{:S(2)}) copy-start(f32[2,128]{1,0:T(2,128)} %gain_ref.1) | copy-start | bytes 3076

commit v3 on v2

--- a/solution.py
+++ b/solution.py
@@ -17,7 +17,7 @@
     return jnp.tanh(half_x) + 1.0
 
 
-PER = 16
+PER = 8
 PAD = 1
 
 
@@ -51,20 +51,21 @@
     return jnp.concatenate(columns, axis=1)
 
 
-def halves_weights(proj_ref, gate_ref, layer):
+def stacked_weights(proj_ref, gate_ref, closer_ref, layer):
     half = jnp.asarray(0.5, jnp.bfloat16)
-    return (proj_ref[layer] * half).T, (gate_ref[layer] * half).T
+    return jnp.concatenate(
+        [(ref[layer] * half).T for ref in (proj_ref, gate_ref, closer_ref)], axis=0
+    )
 
 
 def project_chunk(chunk, normed, mask, weights, scratch):
-    normed = (normed * mask).astype(jnp.bfloat16)
-    projected = jnp.dot(weights[0], normed, preferred_element_type=jnp.float32)
-    gating = jnp.dot(weights[1], normed, preferred_element_type=jnp.float32)
-    halves = double_sigmoid(gating) * projected
-    rows = halves.shape[0]
+    product = jnp.dot(weights, normed.astype(jnp.bfloat16), preferred_element_type=jnp.float32)
+    rows = (product.shape[0] - normed.shape[0]) // 2
+    halves = double_sigmoid(product[rows : 2 * rows]) * (product[:rows] * mask)
     for q in range(PER):
         first = (chunk * PER + q) * (rows + PAD)
         scratch[first : first + rows, :] = halves[:, q * LANES : (q + 1) * LANES]
+    return double_sigmoid(product[2 * rows :]).astype(jnp.bfloat16)
 
 
 def spread_halves(scratch, halves_ref, devices):
@@ -114,9 +115,8 @@
 
     half = jnp.asarray(0.5, jnp.bfloat16)
     turned_ref[0] = (final_ref[0] * half).T
-    turned_ref[1] = (closer_ref[1] * half).T
-    turned_ref[2] = (final_ref[1] * half).T
-    weights_ref[0], weights_ref[1] = halves_weights(proj_ref, gate_ref, 1)
+    turned_ref[1] = (final_ref[1] * half).T
+    weights_ref[...] = stacked_weights(proj_ref, gate_ref, closer_ref, 1)
     table = [
         (out_gain_ref, 0), (out_bias_ref, 0), (gain_ref, 1), (bias_ref, 1), (out_gain_ref, 1),
         (out_bias_ref, 1),
@@ -124,22 +124,15 @@
     for n, (ref, layer) in enumerate(table):
         rows_ref[n : n + 1, :] = ref[layer : layer + 1, :]
 
-    weights = halves_weights(proj_ref, gate_ref, 0)
-    closer = (closer_ref[0] * half).T
+    weights = stacked_weights(proj_ref, gate_ref, closer_ref, 0)
     gain_col = column(gain_ref[0:1, :], PER * LANES)
     bias_col = column(bias_ref[0:1, :], PER * LANES)
     for chunk in range(lane_rows // PER):
         z = load_down(z_ref, chunk, groups)
         z_down_ref[chunk] = z.astype(jnp.bfloat16)
         normed = normalize_down(z, gain_col, bias_col)
-        closing_ref[chunk] = gate_chunk(closer, normed)
-        project_chunk(chunk, normed, mask_ref[chunk], weights, scratch)
+        closing_ref[chunk] = project_chunk(chunk, normed, mask_ref[chunk], weights, scratch)
     spread_halves(scratch, halves_ref, range(halves_ref.shape[0]))
-
-
-def gate_chunk(weight, normed):
-    gating = jnp.dot(weight, normed.astype(jnp.bfloat16), preferred_element_type=jnp.float32)
-    return double_sigmoid(gating).astype(jnp.bfloat16)
 
 
 def finish_chunk(chunk, lane_rows, sums_scratch, gain_col, bias_col, final, closing_ref, z_down_ref):
@@ -172,8 +165,8 @@
 ):
     lane_rows = sums_ref.shape[2]
     load_sums(sums_ref, sums_scratch)
-    final, closer = turned_ref[0], turned_ref[1]
-    weights = weights_ref[0], weights_ref[1]
+    final = turned_ref[0]
+    weights = weights_ref[...]
     out_gain_col, out_bias_col, gain_col, bias_col = [
         column(rows_ref[n : n + 1, :], PER * LANES) for n in range(4)
     ]
@@ -184,8 +177,7 @@
         )
         z_out_ref[chunk] = z
         normed = normalize_down(z.astype(jnp.float32), gain_col, bias_col)
-        closing_out_ref[chunk] = gate_chunk(closer, normed)
-        project_chunk(chunk, normed, mask_ref[chunk], weights, scratch)
+        closing_out_ref[chunk] = project_chunk(chunk, normed, mask_ref[chunk], weights, scratch)
     spread_halves(scratch, halves_ref, range(halves_ref.shape[0]))
 
 
@@ -195,7 +187,7 @@
     lane_rows = sums_ref.shape[2]
     cols = LANES // groups
     load_sums(sums_ref, sums_scratch)
-    final = turned_ref[2]
+    final = turned_ref[1]
     gain_col, bias_col = [column(rows_ref[n : n + 1, :], PER * LANES) for n in (4, 5)]
     copies = []
     for chunk in range(lane_rows // PER):
@@ -324,8 +316,8 @@
             mask_type,
             down_type,
             down_type,
-            jax.ShapeDtypeStruct((3, channels, hidden), jnp.bfloat16),
-            jax.ShapeDtypeStruct((2, 2 * hidden, channels), jnp.bfloat16),
+            jax.ShapeDtypeStruct((2, channels, hidden), jnp.bfloat16),
+            jax.ShapeDtypeStruct((4 * hidden + channels, channels), jnp.bfloat16),
             jax.ShapeDtypeStruct((8, channels), jnp.float32),
         ),
         in_specs=vmem(11),

time: 107 us -> 107 us (level)
  no operation moved by 1% of the time
where the time goes in v3:
time: 107 us; the launch traced here: 106 us
  blocking collectives  99.1 us (93%)
  Pallas kernels  6.03 us (6%)
  local copies, waits for them, and re-layouts  1.18 us (1%)
    all_to_all x4, blocking collectives, exchange(): lax.all_to_all(value, ('row', 'col'), split_axis=0, concat_axis=0, tiled=...  99.1 us

profile of v3, /device:TPU:1, one launch (start us, length us, event | category | flops | bytes accessed | tf_op | source)
XLA Modules:
  0.0 106.4 jit_solution(16017996921947857263)
XLA Ops:
  0.0 0.0 copy-start.3
  0.0 0.0 copy-start.4
  0.0 0.0 copy-start.2
  0.0 0.0 copy-start.1
  0.0 0.0 copy-start
  0.0 0.0 copy-start.6
  0.0 0.0 copy-start.7
  0.0 0.0 copy-start.8
  0.1 0.0 copy-start.9
  0.1 0.0 copy-start.5
  0.1 0.7 copy-done.3
  0.8 0.0 copy-done.4
  0.9 0.1 copy-done.2
  1.0 0.1 copy-done.1
  1.0 0.2 copy-done
  1.2 0.0 copy-done.6
  1.2 0.0 copy-done.7
  1.3 0.0 copy-done.8
  1.3 0.0 copy-done.9
  1.3 0.0 copy-done.5
  1.3 1.4 %shard_map.101 = (bf16[32,8,16,128]{3,2,1,0:T(8,128)(2,1)S(1)}, f32[2,1,1024]{2,1,0:T(1,128)S(1)}, bf16[2,128,1024]{2,1,0:T(8,128)(2,1)S(1)}, bf16[2,128,1024]{2...) custom-call(s32[8,128]{1,0:T(8,128)S(1)} %shard_map.100.slots_ref, ...), custom_call_target="tpu_custom_call" | custom-call | tf_op jit(solution)/shard_map/pallas_call | solution.py:312
  2.7 33.3 %all_to_all.20.halves_ref = bf16[32,8,16,128]{3,2,1,0:T(8,128)(2,1)S(1)} all-to-all(bf16[32,8,16,128]{3,2,1,0:T(8,128)(2,1)S(1)} %get-tuple-element.16), channel_id=1, replica_groups=mesh['row'=8,'col'=4] {'row','col'}, dimensions={0} | all-to-all | bytes 2097152 | tf_op jit(solution)/shard_map/all_to_all | solution.py:291
  36.0 0.5 shard_map.102
  36.5 18.3 %all_to_all.21.sums_ref = bf16[32,4,16,128]{3,2,1,0:T(8,128)(2,1)S(1)} all-to-all(bf16[32,4,16,128]{3,2,1,0:T(8,128)(2,1)S(1)} %shard_map.102), channel_id=1, replica_groups=mesh['row'=8,'col'=4] {'row','col'}, dimensions={0} | all-to-all | bytes 1048576 | tf_op jit(solution)/shard_map/all_to_all | solution.py:291
  54.8 1.9 %shard_map.103 = (bf16[32,8,16,128]{3,2,1,0:T(8,128)(2,1)S(1)}, bf16[2,128,1024]{2,1,0:T(8,128)(2,1)S(1)}, bf16[2,128,1024]{2,1,0:T(8,128)(2,1)S(1)}) custom-call(bf16[2,128,1024]{2,1,0:T(8,128)(2,1)S(1)} %get-tuple-element.15.z_down_ref, bf16[32,4,16,128]{3,2,1,0:T(8,128)(2,1)S(1)} %all_to_all.21.sums_ref, ...), custom_call_target="tpu_custom_call" | custom-call | tf_op jit(solution)/shard_map/pallas_call | solution.py:330
  56.6 29.3 %all_to_all.22.halves_ref = bf16[32,8,16,128]{3,2,1,0:T(8,128)(2,1)S(1)} all-to-all(bf16[32,8,16,128]{3,2,1,0:T(8,128)(2,1)S(1)} %get-tuple-element.23), channel_id=1, replica_groups=mesh['row'=8,'col'=4] {'row','col'}, dimensions={0} | all-to-all | bytes 2097152 | tf_op jit(solution)/shard_map/all_to_all | solution.py:291
  86.0 0.7 shard_map.104
  86.7 18.3 %all_to_all.23.sums_ref = bf16[32,4,16,128]{3,2,1,0:T(8,128)(2,1)S(1)} all-to-all(bf16[32,4,16,128]{3,2,1,0:T(8,128)(2,1)S(1)} %shard_map.104), channel_id=1, replica_groups=mesh['row'=8,'col'=4] {'row','col'}, dimensions={0} | all-to-all | bytes 1048576 | tf_op jit(solution)/shard_map/all_to_all | solution.py:291
  104.9 1.5 %shard_map.105 = bf16[32,64,128]{2,1,0:T(8,128)(2,1)} custom-call(bf16[2,128,1024]{2,1,0:T(8,128)(2,1)S(1)} %get-tuple-element.22.z_down_ref, bf16[32,4,16,128]{3,2,1,0:T(8,128)(2,1)S(1)} %all_to_all.23.sums_ref, bf16[2,128,1024]{2,1,0:T(8,128)(2,1)S(1)} %get-tuple-element.24.closing_ref, bf16[2,128,128]{2,1,0:T(8,128)(2,1)S(1)} %get-tuple-element.18.turned_ref, ...), custom_call_target="tpu_custom_call" | custom-call | tf_op jit(solution)/shard_map/pallas_call | solution.py:339
  (1 shorter events, 0.0 us)
Async XLA Ops:
  0.0 0.8 copy-start.3
  0.0 0.9 copy-start.4
  0.0 1.0 copy-start.2
  0.0 1.0 copy-start.1
  0.0 1.2 %copy-start = (bf16[32,64,128]{2,1,0:T(8,128)(2,1)S(1)}, bf16[32,64,128]{2,1,0:T(8,128)(2,1)}, u32[]{:S(2)}) copy-start(bf16[32,64,128]{2,1,0:T(8,128)(2,1)} %z_ref.1) | copy-start | bytes 1572868
  0.0 1.2 %copy-start.6 = (f32[2,128]{1,0:T(2,128)S(1)}, f32[2,128]{1,0:T(2,128)}, u32[]{:S(2)}) copy-start(f32[2,128]{1,0:T(2,128)} %bias_ref.1) | copy-start | bytes 3076
  0.0 1.2 %copy-start.7 = (s32[256]{0:T(256)S(1)}, s32[256]{0:T(256)}, u32[]{:S(2)}) copy-start(s32[256]{0:T(256)} %param.11) | copy-start | bytes 3076
  0.0 1.2 %copy-start.8 = (f32[2,128]{1,0:T(2,128)S(1)}, f32[2,128]{1,0:T(2,128)}, u32[]{:S(2)}) copy-start(f32[2,128]{1,0:T(2,128)} %out_gain_ref.1) | copy-start | bytes 3076
  0.1 1.2 %copy-start.9 = (f32[2,128]{1,0:T(2,128)S(1)}, f32[2,128]{1,0:T(2,128)}, u32[]{:S(2)}) copy-start(f32[2,128]{1,0:T(2,128)} %out_bias_ref.1) | copy-start | bytes 3076
  0.1 1.2 %copy-start.5 = (f32[2,128]{1,0:T(2,128)S(1)}, f32[2,128]{1,0:T(2,128)}, u32[]{:S(2)}) copy-start(f32[2,128]{1,0:T(2,128)} %gain_ref.1) | copy-start | bytes 3076

commit v4 on v2

--- a/solution.py
+++ b/solution.py
@@ -17,7 +17,7 @@
     return jnp.tanh(half_x) + 1.0
 
 
-PER = 16
+PER = 8
 PAD = 1
 
 
@@ -29,7 +29,8 @@
 
 
 def column(row, width):
-    return jnp.broadcast_to(row, (width, row.shape[1])).T
+    turned = jnp.broadcast_to(row, (LANES, row.shape[1])).T
+    return jnp.concatenate([turned] * (width // LANES), axis=1)
 
 
 def group_at(slot, groups):

time: 107 us -> 107 us (level)
  no operation moved by 1% of the time
where the time goes in v4:
time: 107 us; the launch traced here: 106 us
  blocking collectives  99.1 us (93%)
  Pallas kernels  6.03 us (6%)
  local copies, waits for them, and re-layouts  1.18 us (1%)
    all_to_all x4, blocking collectives, exchange(): lax.all_to_all(value, ('row', 'col'), split_axis=0, concat_axis=0, tiled=...  99.1 us

profile of v4, /device:TPU:1, one launch (start us, length us, event | category | flops | bytes accessed | tf_op | source)
XLA Modules:
  0.0 106.4 jit_solution(17814331966636621516)
XLA Ops:
  0.0 0.0 copy-start.3
  0.0 0.0 copy-start.4
  0.0 0.0 copy-start.2
  0.0 0.0 copy-start.1
  0.0 0.0 copy-start
  0.0 0.0 copy-start.6
  0.0 0.0 copy-start.7
  0.0 0.0 copy-start.8
  0.1 0.0 copy-start.9
  0.1 0.0 copy-start.5
  0.1 0.7 copy-done.3
  0.8 0.0 copy-done.4
  0.9 0.1 copy-done.2
  1.0 0.1 copy-done.1
  1.0 0.2 copy-done
  1.2 0.0 copy-done.6
  1.2 0.0 copy-done.7
  1.3 0.0 copy-done.8
  1.3 0.0 copy-done.9
  1.3 0.0 copy-done.5
  1.3 1.3 %shard_map.101 = (bf16[32,8,16,128]{3,2,1,0:T(8,128)(2,1)S(1)}, f32[2,1,1024]{2,1,0:T(1,128)S(1)}, bf16[2,128,1024]{2,1,0:T(8,128)(2,1)S(1)}, bf16[2,128,1024]{2...) custom-call(s32[8,128]{1,0:T(8,128)S(1)} %shard_map.100.slots_ref, ...), custom_call_target="tpu_custom_call" | custom-call | tf_op jit(solution)/shard_map/pallas_call | solution.py:321
  2.6 33.3 %all_to_all.20.halves_ref = bf16[32,8,16,128]{3,2,1,0:T(8,128)(2,1)S(1)} all-to-all(bf16[32,8,16,128]{3,2,1,0:T(8,128)(2,1)S(1)} %get-tuple-element.16), channel_id=1, replica_groups=mesh['row'=8,'col'=4] {'row','col'}, dimensions={0} | all-to-all | bytes 2097152 | tf_op jit(solution)/shard_map/all_to_all | solution.py:300
  35.9 0.5 shard_map.102
  36.4 18.3 %all_to_all.21.sums_ref = bf16[32,4,16,128]{3,2,1,0:T(8,128)(2,1)S(1)} all-to-all(bf16[32,4,16,128]{3,2,1,0:T(8,128)(2,1)S(1)} %shard_map.102), channel_id=1, replica_groups=mesh['row'=8,'col'=4] {'row','col'}, dimensions={0} | all-to-all | bytes 1048576 | tf_op jit(solution)/shard_map/all_to_all | solution.py:300
  54.7 2.0 %shard_map.103 = (bf16[32,8,16,128]{3,2,1,0:T(8,128)(2,1)S(1)}, bf16[2,128,1024]{2,1,0:T(8,128)(2,1)S(1)}, bf16[2,128,1024]{2,1,0:T(8,128)(2,1)S(1)}) custom-call(bf16[2,128,1024]{2,1,0:T(8,128)(2,1)S(1)} %get-tuple-element.15.z_down_ref, bf16[32,4,16,128]{3,2,1,0:T(8,128)(2,1)S(1)} %all_to_all.21.sums_ref, ...), custom_call_target="tpu_custom_call" | custom-call | tf_op jit(solution)/shard_map/pallas_call | solution.py:339
  56.7 29.3 %all_to_all.22.halves_ref = bf16[32,8,16,128]{3,2,1,0:T(8,128)(2,1)S(1)} all-to-all(bf16[32,8,16,128]{3,2,1,0:T(8,128)(2,1)S(1)} %get-tuple-element.23), channel_id=1, replica_groups=mesh['row'=8,'col'=4] {'row','col'}, dimensions={0} | all-to-all | bytes 2097152 | tf_op jit(solution)/shard_map/all_to_all | solution.py:300
  86.0 0.7 shard_map.104
  86.7 18.3 %all_to_all.23.sums_ref = bf16[32,4,16,128]{3,2,1,0:T(8,128)(2,1)S(1)} all-to-all(bf16[32,4,16,128]{3,2,1,0:T(8,128)(2,1)S(1)} %shard_map.104), channel_id=1, replica_groups=mesh['row'=8,'col'=4] {'row','col'}, dimensions={0} | all-to-all | bytes 1048576 | tf_op jit(solution)/shard_map/all_to_all | solution.py:300
  104.9 1.5 %shard_map.105 = bf16[32,64,128]{2,1,0:T(8,128)(2,1)} custom-call(bf16[2,128,1024]{2,1,0:T(8,128)(2,1)S(1)} %get-tuple-element.22.z_down_ref, bf16[32,4,16,128]{3,2,1,0:T(8,128)(2,1)S(1)} %all_to_all.23.sums_ref, bf16[2,128,1024]{2,1,0:T(8,128)(2,1)S(1)} %get-tuple-element.24.closing_ref, bf16[3,128,128]{2,1,0:T(8,128)(2,1)S(1)} %get-tuple-element.18.turned_ref, ...), custom_call_target="tpu_custom_call" | custom-call | tf_op jit(solution)/shard_map/pallas_call | solution.py:348
  (1 shorter events, 0.0 us)
Async XLA Ops:
  0.0 0.8 copy-start.3
  0.0 0.9 copy-start.4
  0.0 1.0 copy-start.2
  0.0 1.0 copy-start.1
  0.0 1.2 %copy-start = (bf16[32,64,128]{2,1,0:T(8,128)(2,1)S(1)}, bf16[32,64,128]{2,1,0:T(8,128)(2,1)}, u32[]{:S(2)}) copy-start(bf16[32,64,128]{2,1,0:T(8,128)(2,1)} %z_ref.1) | copy-start | bytes 1572868
  0.0 1.2 %copy-start.6 = (f32[2,128]{1,0:T(2,128)S(1)}, f32[2,128]{1,0:T(2,128)}, u32[]{:S(2)}) copy-start(f32[2,128]{1,0:T(2,128)} %bias_ref.1) | copy-start | bytes 3076
  0.0 1.2 %copy-start.7 = (s32[256]{0:T(256)S(1)}, s32[256]{0:T(256)}, u32[]{:S(2)}) copy-start(s32[256]{0:T(256)} %param.11) | copy-start | bytes 3076
  0.0 1.2 %copy-start.8 = (f32[2,128]{1,0:T(2,128)S(1)}, f32[2,128]{1,0:T(2,128)}, u32[]{:S(2)}) copy-start(f32[2,128]{1,0:T(2,128)} %out_gain_ref.1) | copy-start | bytes 3076
  0.1 1.2 %copy-start.9 = (f32[2,128]{1,0:T(2,128)S(1)}, f32[2,128]{1,0:T(2,128)}, u32[]{:S(2)}) copy-start(f32[2,128]{1,0:T(2,128)} %out_bias_ref.1) | copy-start | bytes 3076
  0.1 1.2 %copy-start.5 = (f32[2,128]{1,0:T(2,128)S(1)}, f32[2,128]{1,0:T(2,128)}, u32[]{:S(2)}) copy-start(f32[2,128]{1,0:T(2,128)} %gain_ref.1) | copy-start | bytes 3076

commit v5 on v3

--- a/solution.py
+++ b/solution.py
@@ -29,7 +29,8 @@
 
 
 def column(row, width):
-    return jnp.broadcast_to(row, (width, row.shape[1])).T
+    turned = jnp.broadcast_to(row, (LANES, row.shape[1])).T
+    return jnp.concatenate([turned] * (width // LANES), axis=1)
 
 
 def group_at(slot, groups):
@@ -83,13 +84,11 @@
     slots_ref[...] = lax.broadcasted_iota(jnp.int32, slots_ref.shape, 1) // cols
 
 
-def first_kernel(
-    groups, slots_ref, z_ref, gain_ref, bias_ref, proj_ref, gate_ref, mask_row_ref, closer_ref,
-    out_gain_ref, out_bias_ref, final_ref,
-    halves_ref, mask_ref, z_down_ref, closing_ref, turned_ref, weights_ref, rows_ref,
-    mask_col_ref, scratch,
-):
-    rows, cols, _ = z_ref.shape
+def prepare_kernel(
+    groups, rows, cols, slots_ref, gain_ref, bias_ref, proj_ref, gate_ref, mask_row_ref,
+    closer_ref, out_gain_ref, out_bias_ref, final_ref,
+    mask_ref, turned_ref, weights_ref, rows_ref, mask_col_ref,
+):
     tokens = mask_row_ref.shape[1]
     lane_rows = rows // groups
 
@@ -116,17 +115,22 @@
     half = jnp.asarray(0.5, jnp.bfloat16)
     turned_ref[0] = (final_ref[0] * half).T
     turned_ref[1] = (final_ref[1] * half).T
-    weights_ref[...] = stacked_weights(proj_ref, gate_ref, closer_ref, 1)
+    for layer in range(2):
+        weights_ref[layer] = stacked_weights(proj_ref, gate_ref, closer_ref, layer)
     table = [
         (out_gain_ref, 0), (out_bias_ref, 0), (gain_ref, 1), (bias_ref, 1), (out_gain_ref, 1),
-        (out_bias_ref, 1),
+        (out_bias_ref, 1), (gain_ref, 0), (bias_ref, 0),
     ]
     for n, (ref, layer) in enumerate(table):
         rows_ref[n : n + 1, :] = ref[layer : layer + 1, :]
 
-    weights = stacked_weights(proj_ref, gate_ref, closer_ref, 0)
-    gain_col = column(gain_ref[0:1, :], PER * LANES)
-    bias_col = column(bias_ref[0:1, :], PER * LANES)
+
+def first_kernel(
+    groups, z_ref, mask_ref, weights_ref, rows_ref, halves_ref, z_down_ref, closing_ref, scratch
+):
+    lane_rows = z_ref.shape[0] // groups
+    weights = weights_ref[0]
+    gain_col, bias_col = [column(rows_ref[n : n + 1, :], PER * LANES) for n in (6, 7)]
     for chunk in range(lane_rows // PER):
         z = load_down(z_ref, chunk, groups)
         z_down_ref[chunk] = z.astype(jnp.bfloat16)
@@ -166,7 +170,7 @@
     lane_rows = sums_ref.shape[2]
     load_sums(sums_ref, sums_scratch)
     final = turned_ref[0]
-    weights = weights_ref[...]
+    weights = weights_ref[1]
     out_gain_col, out_bias_col, gain_col, bias_col = [
         column(rows_ref[n : n + 1, :], PER * LANES) for n in range(4)
     ]
@@ -309,23 +313,28 @@
             flops=10**9, bytes_accessed=8 * LANES * 4, transcendentals=0
         ),
     )()
-    halves, mask, z_down, closing, turned, weights, table = pl.pallas_call(
-        functools.partial(first_kernel, groups),
+    mask, turned, weights, table = pl.pallas_call(
+        functools.partial(prepare_kernel, groups, rows, cols),
         out_shape=(
-            halves_type,
             mask_type,
-            down_type,
-            down_type,
             jax.ShapeDtypeStruct((2, channels, hidden), jnp.bfloat16),
-            jax.ShapeDtypeStruct((4 * hidden + channels, channels), jnp.bfloat16),
+            jax.ShapeDtypeStruct((2, 4 * hidden + channels, channels), jnp.bfloat16),
             jax.ShapeDtypeStruct((8, channels), jnp.float32),
         ),
-        in_specs=vmem(11),
-        out_specs=tuple(vmem(7)),
-        scratch_shapes=[pltpu.VMEM((tokens, LANES), jnp.float32), halves_scratch],
+        in_specs=vmem(10),
+        out_specs=tuple(vmem(4)),
+        scratch_shapes=[pltpu.VMEM((tokens, LANES), jnp.float32)],
         compiler_params=params,
-    )(slots, pair_map, norm_gain, norm_bias, proj_weight, gate_weight,
-      token_mask.reshape(1, tokens), output_gate, out_gain, out_bias, final_weight)
+    )(slots, norm_gain, norm_bias, proj_weight, gate_weight, token_mask.reshape(1, tokens),
+      output_gate, out_gain, out_bias, final_weight)
+    halves, z_down, closing = pl.pallas_call(
+        functools.partial(first_kernel, groups),
+        out_shape=(halves_type, down_type, down_type),
+        in_specs=vmem(4),
+        out_specs=tuple(vmem(3)),
+        scratch_shapes=[halves_scratch],
+        compiler_params=params,
+    )(pair_map, mask, weights, table)
     sums = exchange(triangle(0, exchange(halves)))
     halves, z_down, closing = pl.pallas_call(
         middle_kernel,

time: 107 us -> 107 us (level)
  no operation moved by 1% of the time
where the time goes in v5:
time: 107 us; the launch traced here: 106 us
  blocking collectives  99.1 us (93%)
  Pallas kernels  6.19 us (6%)
    all_to_all x4, blocking collectives, exchange(): lax.all_to_all(value, ('row', 'col'), split_axis=0, concat_axis=0, tiled=...  99.1 us

profile of v5, /device:TPU:1, one launch (start us, length us, event | category | flops | bytes accessed | tf_op | source)
XLA Modules:
  0.0 106.4 jit_solution(17094761455075104826)
XLA Ops:
  0.0 0.0 copy-start.3
  0.0 0.0 copy-start.4
  0.0 0.0 copy-start.2
  0.0 0.0 copy-start.1
  0.0 0.0 copy-start.6
  0.0 0.0 copy-start.7
  0.0 0.0 copy-start.8
  0.0 0.0 copy-start.9
  0.1 0.0 copy-start
  0.1 0.0 copy-start.5
  0.1 0.7 copy-done.3
  0.8 0.0 copy-done.4
  0.9 0.1 copy-done.2
  1.0 0.1 copy-done.1
  1.0 0.0 copy-done.6
  1.0 0.0 copy-done.7
  1.0 0.0 copy-done.8
  1.0 0.0 copy-done.9
  1.1 0.0 copy-done.5
  1.1 0.3 shard_map.101
  1.3 0.0 copy-done
  1.3 1.3 %shard_map.102 = (bf16[32,8,16,128]{3,2,1,0:T(8,128)(2,1)S(1)}, bf16[2,128,1024]{2,1,0:T(8,128)(2,1)S(1)}, bf16[2,128,1024]{2,1,0:T(8,128)(2,1)S(1)}) custom-call(bf16[32,64,128]{2,1,0:T(8,128)(2,1)S(1)} %copy-done, f32[2,1,1024]{2,1,0:T(1,128)S(1)} %get-tuple-element.15.mask_ref, bf16[2,640,128]{2,1,0:T(8,128)(2,1)S(1)} %get-tuple-element.16.weights_ref, ...), custom_call_target="tpu_custom_call" | custom-call | tf_op jit(solution)/shard_map/pallas_call | solution.py:330
  2.7 33.3 %all_to_all.20.halves_ref = bf16[32,8,16,128]{3,2,1,0:T(8,128)(2,1)S(1)} all-to-all(bf16[32,8,16,128]{3,2,1,0:T(8,128)(2,1)S(1)} %get-tuple-element.19), channel_id=1, replica_groups=mesh['row'=8,'col'=4] {'row','col'}, dimensions={0} | all-to-all | bytes 2097152 | tf_op jit(solution)/shard_map/all_to_all | solution.py:295
  35.9 0.5 shard_map.103
  36.5 18.3 %all_to_all.21.sums_ref = bf16[32,4,16,128]{3,2,1,0:T(8,128)(2,1)S(1)} all-to-all(bf16[32,4,16,128]{3,2,1,0:T(8,128)(2,1)S(1)} %shard_map.103), channel_id=1, replica_groups=mesh['row'=8,'col'=4] {'row','col'}, dimensions={0} | all-to-all | bytes 1048576 | tf_op jit(solution)/shard_map/all_to_all | solution.py:295
  54.7 1.9 %shard_map.104 = (bf16[32,8,16,128]{3,2,1,0:T(8,128)(2,1)S(1)}, bf16[2,128,1024]{2,1,0:T(8,128)(2,1)S(1)}, bf16[2,128,1024]{2,1,0:T(8,128)(2,1)S(1)}) custom-call(bf16[2,128,1024]{2,1,0:T(8,128)(2,1)S(1)} %get-tuple-element.18.z_down_ref, bf16[32,4,16,128]{3,2,1,0:T(8,128)(2,1)S(1)} %all_to_all.21.sums_ref, ...), custom_call_target="tpu_custom_call" | custom-call | tf_op jit(solution)/shard_map/pallas_call | solution.py:339
  56.6 29.3 %all_to_all.22.halves_ref = bf16[32,8,16,128]{3,2,1,0:T(8,128)(2,1)S(1)} all-to-all(bf16[32,8,16,128]{3,2,1,0:T(8,128)(2,1)S(1)} %get-tuple-element.23), channel_id=1, replica_groups=mesh['row'=8,'col'=4] {'row','col'}, dimensions={0} | all-to-all | bytes 2097152 | tf_op jit(solution)/shard_map/all_to_all | solution.py:295
  85.9 0.7 shard_map.105
  86.6 18.3 %all_to_all.23.sums_ref = bf16[32,4,16,128]{3,2,1,0:T(8,128)(2,1)S(1)} all-to-all(bf16[32,4,16,128]{3,2,1,0:T(8,128)(2,1)S(1)} %shard_map.105), channel_id=1, replica_groups=mesh['row'=8,'col'=4] {'row','col'}, dimensions={0} | all-to-all | bytes 1048576 | tf_op jit(solution)/shard_map/all_to_all | solution.py:295
  104.9 1.5 %shard_map.106 = bf16[32,64,128]{2,1,0:T(8,128)(2,1)} custom-call(bf16[2,128,1024]{2,1,0:T(8,128)(2,1)S(1)} %get-tuple-element.22.z_down_ref, bf16[32,4,16,128]{3,2,1,0:T(8,128)(2,1)S(1)} %all_to_all.23.sums_ref, bf16[2,128,1024]{2,1,0:T(8,128)(2,1)S(1)} %get-tuple-element.24.closing_ref, bf16[2,128,128]{2,1,0:T(8,128)(2,1)S(1)} %get-tuple-element.21.turned_ref, ...), custom_call_target="tpu_custom_call" | custom-call | tf_op jit(solution)/shard_map/pallas_call | solution.py:348
  (1 shorter events, 0.0 us)
Async XLA Ops:
  0.0 0.8 copy-start.3
  0.0 0.9 copy-start.4
  0.0 1.0 copy-start.2
  0.0 1.0 copy-start.1
  0.0 1.0 copy-start.6
  0.0 1.0 copy-start.7
  0.0 1.0 copy-start.8
  0.0 1.0 copy-start.9
  0.1 1.3 %copy-start = (bf16[32,64,128]{2,1,0:T(8,128)(2,1)S(1)}, bf16[32,64,128]{2,1,0:T(8,128)(2,1)}, u32[]{:S(2)}) copy-start(bf16[32,64,128]{2,1,0:T(8,128)(2,1)} %z_ref.1) | copy-start | bytes 1572868
  0.1 1.0 copy-start.5
